TPU v7x, 32 devices: a whole 2x2x4 slice. The times are simulated.
32 devices in a mesh: shard: 4 (over z), tensor: 4 (over y, x), section: 2 (over core).
Axes of the slice: x: 2, y: 2, z: 4, core: 2. Of those that a mesh axis runs over, the one named last changes fastest.
Arguments:
- grad_parts: bfloat16 [4, 2, 4, 1024, 1024], P('shard', 'section', None, 'tensor'), may hold values from -45 to 45
- vector_grads: bfloat16 [4, 2, 4, 1024], P('shard', 'section', None, 'tensor'), may hold values from -6 to 6
- momentum: float32 [2, 4, 1024, 1024], P('section', None, ('tensor', 'shard')), may hold values from -6 to 6
- weights: bfloat16 [2, 4, 1024, 1024], P('section', None, ('tensor', 'shard')), may hold values from -0.1875 to 0.1875
- vectors: float32 [2, 4, 1024], P('section', None, ('tensor', 'shard')), may hold values from 0.5 to 1.5
- first_moment: float32 [2, 4, 1024], P('section', None, ('tensor', 'shard')), may hold values from -3 to 3
- second_moment: float32 [2, 4, 1024], P('section', None, ('tensor', 'shard')), may hold values from 0.05 to 2
Outputs:
- new_momentum: float32 [2, 4, 1024, 1024], P('section', None, ('tensor', 'shard'))
- orthogonal_update: bfloat16 [2, 4, 1024, 1024], P('section', None, ('tensor', 'shard'))
- new_weights: bfloat16 [2, 4, 1024, 1024], P('section', None, ('tensor', 'shard'))
- adam_direction: float32 [2, 4, 1024], P('section', None, ('tensor', 'shard'))
- new_vectors: float32 [2, 4, 1024], P('section', None, ('tensor', 'shard'))
All inputs are finite; a program needn't handle non-finite values.
Results may differ from a plain program's by a relative error of at most 0.0048.
The roundings to bfloat16 on the way count: a program that leaves them out, or rounds other values in their place, can miss the bound.
Values may be sent and summed in bfloat16 or wider, within the bound.
No kernel may reach another device: no remote copies, remote signals or barrier semaphores. Data moves between devices by JAX's collectives and lax.ppermute only.
A program may use at most 64 MiB of HBM per device.

v0:
```python
import functools
import math

import jax
import jax.numpy as jnp
from jax import lax
from jax.experimental import pallas as pl
from jax.experimental.pallas import tpu as pltpu
from jax.sharding import PartitionSpec as P

D = 1024
NS_STEPS = 2


ns_first = 3.4445
ns_second = -4.775
ns_third = 2.0315
mom_beta = 0.95
max_norm = 1024.0
muon_rate = 0.02
muon_decay = 0.1
adam_rate = 0.001
adam_decay = 0.01

VECTOR_ROWS = 16
FIGURES = 16
LANES = 128
MESH_AXES = ("shard", "tensor", "section")


def gram_of(blocks, gram_ref):
    width = blocks[0].shape[1]
    step = 256
    for start in range(0, width, step):
        total = None
        for block in blocks:
            whole = block[...]
            part = whole[:, start : start + step]
            product = lax.dot_general(
                whole, part, (((0,), (0,)), ((), ())), preferred_element_type=jnp.float32
            )
            rounded = product.astype(jnp.bfloat16).astype(jnp.float32)
            total = rounded if total is None else total + rounded
        gram_ref[:, start : start + step] = total.astype(jnp.bfloat16)


def polynomial(block, gram_ref):
    gram = gram_ref[...]
    first = jnp.dot(block, gram, preferred_element_type=jnp.float32).astype(jnp.bfloat16)
    second = jnp.dot(first, gram, preferred_element_type=jnp.float32)
    combined = (
        ns_first * block.astype(jnp.float32)
        + ns_second * first.astype(jnp.float32)
        + ns_third * second
    )
    return combined.astype(jnp.bfloat16)


def orthogonalize_kernel(count, pieces, *refs):
    height, width = refs[0].shape
    inputs = refs[: count * pieces]
    outputs = refs[count * pieces : count * pieces + pieces]
    gram_ref, start_ref, next_ref = refs[count * pieces + pieces :]
    for position in range(count):
        for piece in range(pieces):
            start_ref[position, piece * height : (piece + 1) * height, :] = inputs[
                position * pieces + piece
            ][...]
    current, other = start_ref, next_ref
    for iteration in range(NS_STEPS - 1):
        gram_of([current.at[position] for position in range(count)], gram_ref)
        for position in range(count):
            other[position] = polynomial(current[position], gram_ref)
        current, other = other, current
    gram_of([current.at[position] for position in range(count)], gram_ref)
    result = polynomial(current[0], gram_ref)
    for piece in range(pieces):
        outputs[piece][...] = result[piece * height : (piece + 1) * height, :]


def orthogonalize(blocks):
    count, pieces = len(blocks), len(blocks[0])
    height, width = blocks[0][0].shape
    return pl.pallas_call(
        functools.partial(orthogonalize_kernel, count, pieces),
        out_shape=[jax.ShapeDtypeStruct((height, width), jnp.bfloat16)] * pieces,
        scratch_shapes=[
            pltpu.VMEM((width, width), jnp.bfloat16),
            pltpu.VMEM((count, pieces * height, width), jnp.bfloat16),
            pltpu.VMEM((count, pieces * height, width), jnp.bfloat16),
        ],
        compiler_params=pltpu.CompilerParams(vmem_limit_bytes=48 * 2**20),
    )(*[piece for block in blocks for piece in block])


def folded(array):
    line = jnp.sum(array, axis=0, keepdims=True)
    total = line[:, :LANES]
    for start in range(LANES, line.shape[1], LANES):
        total = total + line[:, start : start + LANES]
    return total


def sum_kernel(shard_count, section_ref, *refs):
    parts = refs[:shard_count]
    vector_parts = refs[shard_count : 2 * shard_count]
    momentum_ref, grad_ref, vector_ref, figures_ref = refs[2 * shard_count :]
    vector = vector_parts[0][...].astype(jnp.float32)
    for part in vector_parts[1:]:
        vector = vector + part[...].astype(jnp.float32)
    vector_ref[...] = vector
    total = folded(vector * vector) * (1.0 / shard_count)
    squares, crosses, momentum_squares = [], [], []
    for matrix in range(momentum_ref.shape[0]):
        grad = parts[0][matrix].astype(jnp.float32)
        for part in parts[1:]:
            grad = grad + part[matrix].astype(jnp.float32)
        grad_ref[matrix] = grad
        old = momentum_ref[matrix]
        squares.append(folded(grad * grad))
        crosses.append(folded(grad * old))
        momentum_squares.append(folded(old * old))
        total = total + squares[-1]
    lines = squares + crosses + momentum_squares + [total]
    lines = lines + [jnp.zeros_like(total)] * (FIGURES - len(lines))
    tile = jnp.concatenate(lines, axis=0)
    line_index = lax.broadcasted_iota(jnp.int32, tile.shape, 0)
    total_only = jnp.where(line_index == 3 * momentum_ref.shape[0], tile, 0.0)
    for section in range(figures_ref.shape[1]):
        chosen = jnp.where(section_ref[0] == section, tile, total_only)
        figures_ref[:, section] = jnp.broadcast_to(
            chosen[None], (figures_ref.shape[0],) + tile.shape
        )


def scale_kernel(matrix_count, order_ref, figures_ref, grad_ref, momentum_ref, *refs):
    outputs, clip_ref = refs[:matrix_count], refs[matrix_count]
    sums = jnp.sum(jnp.sum(figures_ref[...], axis=0), axis=1, keepdims=True)
    total = sums[3 * matrix_count : 3 * matrix_count + 1]
    clip = jnp.minimum(1.0, max_norm / (jnp.sqrt(total) + 1e-06))
    clip_ref[...] = jnp.broadcast_to(clip, clip_ref.shape)
    grad_scale = (1.0 + mom_beta) * clip
    momentum_scale = mom_beta * mom_beta
    update_norm = (
        grad_scale * grad_scale * sums[:matrix_count]
        + 2.0 * grad_scale * momentum_scale * sums[matrix_count : 2 * matrix_count]
        + momentum_scale * momentum_scale * sums[2 * matrix_count : 3 * matrix_count]
    )
    inverse = 1.0 / (jnp.sqrt(jnp.maximum(update_norm, 0.0)) + 1e-07)
    position = lax.broadcasted_iota(jnp.int32, inverse.shape, 0)
    for place in range(matrix_count):
        matrix = order_ref[place]
        factor = jnp.sum(jnp.where(position == matrix, inverse, 0.0), axis=0, keepdims=True)
        clipped = clip * grad_ref[matrix]
        nesterov = clipped + mom_beta * (mom_beta * momentum_ref[matrix] + clipped)
        outputs[place][...] = (nesterov * factor).astype(jnp.bfloat16)


def end_kernel(matrix_count, order_ref, *refs):
    arrived = refs[:matrix_count]
    weights_ref, update_ref, new_weights_ref = refs[matrix_count:]
    step_size = muon_rate * (0.2 * math.sqrt(D))
    for place in range(matrix_count):
        matrix = order_ref[place]
        update = arrived[place][...]
        update_ref[matrix] = update
        new_weights_ref[matrix] = (
            weights_ref[matrix].astype(jnp.float32) * (1.0 - muon_rate * muon_decay)
            - step_size * update.astype(jnp.float32)
        ).astype(jnp.bfloat16)


def on_device(kernel, scalars, operands, out_shape):
    return pl.pallas_call(
        kernel,
        out_shape=out_shape,
        in_specs=[pl.BlockSpec(memory_space=pltpu.SMEM)]
        + [pl.BlockSpec(memory_space=pltpu.VMEM)] * len(operands),
        compiler_params=pltpu.CompilerParams(vmem_limit_bytes=32 * 2**20),
    )(scalars, *operands)


def swapped(array, axis, offset):
    pairs = [(i, i ^ offset) for i in range(lax.axis_size(axis))]
    return lax.ppermute(array, axis, pairs)


def per_device(grad_parts, vector_grads, momentum, weights, vectors, first_moment, second_moment):
    shard_count = lax.axis_size("shard")
    tensor_count = lax.axis_size("tensor")
    section_count = lax.axis_size("section")
    _, matrix_count, local_height, width = momentum.shape
    if shard_count != matrix_count or shard_count != 4 or tensor_count != 4:
        return general_device(
            grad_parts, vector_grads, momentum, weights, vectors, first_moment, second_moment
        )
    shard_index = lax.axis_index("shard")
    order = shard_index ^ jnp.arange(shard_count, dtype=jnp.int32)
    own_momentum = momentum[0]
    vector_count, vector_width = vectors.shape[1:]

    by_rows = grad_parts.reshape(matrix_count, shard_count, local_height, width)
    own_vectors = vector_grads.reshape(vector_count, shard_count * vector_width)
    parts = [None] * shard_count
    vector_parts = [own_vectors] + [None] * (shard_count - 1)
    for offset in reversed(range(shard_count)):
        rows = lax.dynamic_index_in_dim(by_rows, shard_index ^ offset, 1, keepdims=False)
        parts[offset] = swapped(rows, "shard", offset) if offset else rows
    for offset in range(1, shard_count):
        vector_parts[offset] = swapped(own_vectors, "shard", offset)

    others = shard_count * tensor_count
    grad_rows, vector_whole, figures = on_device(
        functools.partial(sum_kernel, shard_count),
        lax.axis_index("section").astype(jnp.int32).reshape(1),
        parts + vector_parts + [own_momentum],
        [
            jax.ShapeDtypeStruct(own_momentum.shape, jnp.float32),
            jax.ShapeDtypeStruct(own_vectors.shape, jnp.float32),
            jax.ShapeDtypeStruct((others, section_count, FIGURES, LANES), jnp.float32),
        ],
    )
    figures = lax.all_to_all(
        figures.reshape(others * section_count, FIGURES, LANES),
        MESH_AXES,
        split_axis=0,
        concat_axis=0,
        tiled=True,
    )
    *scaled, clip_tile = on_device(
        functools.partial(scale_kernel, matrix_count),
        order,
        [figures, grad_rows, own_momentum],
        [jax.ShapeDtypeStruct((local_height, width), jnp.bfloat16)] * matrix_count
        + [jax.ShapeDtypeStruct((8, LANES), jnp.float32)],
    )

    blocks = [[], [], [], []]
    for offset in range(shard_count):
        piece = swapped(scaled[offset], "shard", offset) if offset else scaled[0]
        near = swapped(piece, "tensor", 1)
        side = swapped(piece, "tensor", 2)
        far = swapped(near, "tensor", 2) if offset % 2 == 0 else swapped(side, "tensor", 1)
        for block, held in zip(blocks, (piece, near, side, far)):
            block.append(held)
    results = orthogonalize(blocks)

    arrived = [
        swapped(results[offset], "shard", offset) if offset else results[0]
        for offset in range(shard_count)
    ]
    orthogonal_update, new_weights = on_device(
        functools.partial(end_kernel, matrix_count),
        order,
        arrived + [weights[0]],
        [jax.ShapeDtypeStruct(own_momentum.shape, jnp.bfloat16)] * 2,
    )

    clip_factor = clip_tile[0, 0]
    new_momentum = mom_beta * own_momentum + clip_factor * grad_rows
    vector_rows = lax.dynamic_slice_in_dim(
        vector_whole, shard_index * vector_width, vector_width, 1
    )
    vector_clipped = clip_factor * vector_rows
    updated_first = 0.9 * first_moment + 0.1 * vector_clipped
    updated_second = 0.999 * second_moment + 0.001 * vector_clipped * vector_clipped
    adam_direction = updated_first / (jnp.sqrt(updated_second) + 1e-08)
    new_vectors = vectors * (1.0 - adam_rate * adam_decay) - adam_rate * adam_direction
    return (
        new_momentum[None],
        orthogonal_update[None],
        new_weights[None],
        adam_direction,
        new_vectors,
    )


def general_device(grad_parts, vector_grads, momentum, weights, vectors, first_moment, second_moment):
    shard_count = lax.axis_size("shard")
    tensor_count = lax.axis_size("tensor")
    section_count = lax.axis_size("section")
    shard_index = lax.axis_index("shard")
    _, matrix_count, local_height, width = momentum.shape
    vector_width = vectors.shape[2]
    own_momentum = momentum[0]

    rows = matrix_count * local_height
    by_target = (
        grad_parts.reshape(matrix_count, shard_count, local_height, width)
        .transpose(1, 0, 2, 3)
        .reshape(shard_count, rows, width)
    )
    vector_line = jnp.broadcast_to(
        vector_grads.reshape(1, 1, width), (shard_count, VECTOR_ROWS, width)
    )
    payload = jnp.concatenate([by_target, vector_line], axis=1)
    arrived = lax.all_to_all(payload, "shard", split_axis=0, concat_axis=0, tiled=True)
    grad_rows = jnp.sum(arrived[:, :rows].astype(jnp.float32), axis=0).reshape(
        matrix_count, local_height, width
    )
    vector_whole = jnp.sum(arrived[:, rows].astype(jnp.float32), axis=0).reshape(
        vectors.shape[1], vector_width * shard_count
    )
    vector_rows = lax.dynamic_slice_in_dim(
        vector_whole, shard_index * vector_width, vector_width, 1
    )

    grad_squares = jnp.sum(grad_rows * grad_rows, axis=(1, 2))
    cross = jnp.sum(grad_rows * own_momentum, axis=(1, 2))
    momentum_squares = jnp.sum(own_momentum * own_momentum, axis=(1, 2))
    own_total = jnp.sum(grad_squares) + jnp.sum(vector_rows * vector_rows)
    same_section = (
        jnp.arange(section_count) == lax.axis_index("section")
    ).astype(jnp.float32)[:, None]
    matrix_figures = jnp.concatenate([grad_squares, cross, momentum_squares])
    line = jnp.concatenate(
        [
            same_section * matrix_figures[None],
            jnp.broadcast_to(own_total, (section_count, 1)),
            jnp.zeros((section_count, 127 - 3 * matrix_count), jnp.float32),
        ],
        axis=1,
    )
    others = shard_count * tensor_count
    figures = jnp.broadcast_to(line[None, :, None, :], (others, section_count, 8, 128)).reshape(
        others * section_count, 8, 128
    )
    figures = lax.all_to_all(figures, MESH_AXES, split_axis=0, concat_axis=0, tiled=True)
    sums = jnp.sum(figures[:, 0, :], axis=0)
    grand_total = sums[3 * matrix_count]
    clip_factor = jnp.minimum(1.0, max_norm / (jnp.sqrt(grand_total) + 1e-06))
    grad_scale = (1.0 + mom_beta) * clip_factor
    momentum_scale = mom_beta * mom_beta
    update_norm = (
        grad_scale * grad_scale * sums[:matrix_count]
        + 2.0 * grad_scale * momentum_scale * sums[matrix_count : 2 * matrix_count]
        + momentum_scale * momentum_scale * sums[2 * matrix_count : 3 * matrix_count]
    )
    update_norm = jnp.maximum(update_norm, 0.0)[:, None, None]

    new_momentum = mom_beta * own_momentum + clip_factor * grad_rows
    nesterov = clip_factor * grad_rows + mom_beta * new_momentum
    scaled = (nesterov / (jnp.sqrt(update_norm) + 1e-07)).astype(jnp.bfloat16)

    owner_count = shard_count // matrix_count
    if owner_count == 1:
        row_block = lax.all_to_all(scaled, "shard", split_axis=0, concat_axis=0, tiled=True)
        row_block = row_block.reshape(shard_count * local_height, width)
    else:
        everything = lax.all_gather(scaled, "shard", axis=1, tiled=True)
        row_block = lax.dynamic_index_in_dim(
            everything, shard_index // owner_count, 0, keepdims=False
        )

    blocks = [row_block]
    for offset in range(1, tensor_count):
        pairs = [(i, i ^ offset) for i in range(tensor_count)]
        blocks.append(lax.ppermute(row_block, "tensor", pairs))
    (own_result,) = orthogonalize([[block] for block in blocks])

    if owner_count == 1:
        own_update = lax.all_to_all(
            own_result.reshape(shard_count, local_height, width),
            "shard",
            split_axis=0,
            concat_axis=0,
            tiled=True,
        )
    else:
        piece_length = local_height * width // owner_count
        split_rows = own_result.reshape(shard_count, owner_count, piece_length)
        returning = lax.dynamic_index_in_dim(
            split_rows, shard_index % owner_count, 1, keepdims=False
        )
        received = lax.all_to_all(returning, "shard", split_axis=0, concat_axis=0, tiled=True)
        own_update = received.reshape(matrix_count, local_height, width)
    orthogonal_update = own_update[None]
    muon_scale = 0.2 * math.sqrt(D)
    new_weights = (
        weights.astype(jnp.float32) * (1.0 - muon_rate * muon_decay)
        - muon_rate * muon_scale * orthogonal_update.astype(jnp.float32)
    ).astype(jnp.bfloat16)
    vector_clipped = clip_factor * vector_rows
    updated_first = 0.9 * first_moment + 0.1 * vector_clipped
    updated_second = 0.999 * second_moment + 0.001 * vector_clipped * vector_clipped
    adam_direction = updated_first / (jnp.sqrt(updated_second) + 1e-08)
    new_vectors = vectors * (1.0 - adam_rate * adam_decay) - adam_rate * adam_direction
    return (new_momentum[None], orthogonal_update, new_weights, adam_direction, new_vectors)


def solution(mesh):
    in_specs = (
        P("shard", "section", None, "tensor", None),
        P("shard", "section", None, "tensor"),
        P("section", None, ("tensor", "shard"), None),
        P("section", None, ("tensor", "shard"), None),
        P("section", None, ("tensor", "shard")),
        P("section", None, ("tensor", "shard")),
        P("section", None, ("tensor", "shard")),
    )
    out_specs = (
        P("section", None, ("tensor", "shard"), None),
        P("section", None, ("tensor", "shard"), None),
        P("section", None, ("tensor", "shard"), None),
        P("section", None, ("tensor", "shard")),
        P("section", None, ("tensor", "shard")),
    )
    return jax.shard_map(
        per_device, mesh=mesh, in_specs=in_specs, out_specs=out_specs, check_vma=False
    )
```

profile of v0, /device:TPU:0, one launch (start us, length us, event | category | flops | bytes accessed | tf_op | source)
XLA Modules:
  0.0 130.8 jit_solution(14727554777602185778)
XLA Ops:
  0.7 0.0 copy-start.6
  0.7 2.8 %dynamic-slice_bitcast_fusion = (bf16[4,64,1024]{2,1,0:T(8,128)(2,1)}, bf16[4,64,1024]{2,1,0:T(8,128)(2,1)}, bf16[4,64,1024]{2,1,0:T(8,128)(2,1)}, bf16[4,64,1024]{2,1,0:T(8,128)(2,1)S(1)}) fusion(bf16[4,4,64,1024]{3,2,1,0:T(8,128)(2,1)} %bitcast.51, s32[]{:T(128)S(6)} %select_n.19, s32[]{:T(128)S(6)} %select_n.18, s32[]{:T(128)S(6)} %select_n.17, ...), kind=kLoop, calls=%fused_computation.1 | loop fusion | bytes 4194320 | tf_op jit(solution)/shard_map/jit(dynamic_index_in_dim)/squeeze | solution.py:207
  3.5 5.0 %collective-permute-start.2 = (bf16[4,64,1024]{2,1,0:T(8,128)(2,1)}, bf16[4,64,1024]{2,1,0:T(8,128)(2,1)S(1)}, u32[]{:S(2)}, u32[]{:S(2)}) collective-permute-start(bf16[4,64,1024]{2,1,0:T(8,128)(2,1)} %get-tuple-element.35), channel_id=1, source_target_pairs={{0,24},{8,16},{16,8},{24,0},{1,25},{9,17},{17,9},{25,1},{2,26},{10... | collective-permute-start | bytes 1572872 | tf_op jit(solution)/shard_map/ppermute | solution.py:185
  8.5 0.0 collective-permute-start.1
  8.5 0.6 collective-permute-start
  9.1 0.0 copy-done.6
  9.1 3.8 %collective-permute-start.5 = (bf16[4,256]{1,0:T(4,128)(2,1)S(1)}, bf16[4,256]{1,0:T(4,128)(2,1)S(1)}, u32[]{:S(2)}, u32[]{:S(2)}) collective-permute-start(bf16[4,256]{1,0:T(4,128)(2,1)S(1)} %bitcast.47), channel_id=1, source_target_pairs={{0,24},{8,16},{16,8},{24,0},{1,25},{9,17},{17,9},{25,1},{2,26},{10... | collective-permute-start | bytes 6152 | tf_op jit(solution)/shard_map/ppermute | solution.py:185
  12.9 0.0 collective-permute-start.4
  12.9 30.5 %collective-permute-done.5.refs_7_ = bf16[4,256]{1,0:T(4,128)(2,1)S(1)} collective-permute-done((bf16[4,256]{1,0:T(4,128)(2,1)S(1)}, bf16[4,256]{1,0:T(4,128)(2,1)S(1)}, u32[]{:S(2)}, u32[]{:S(2)}) %collective-permute-start.5) | collective-permute-done | bytes 2080 | tf_op jit(solution)/shard_map/ppermute | solution.py:185
  43.4 10.8 %collective-permute-start.3 = (bf16[4,256]{1,0:T(4,128)(2,1)S(1)}, bf16[4,256]{1,0:T(4,128)(2,1)S(1)}, u32[]{:S(2)}, u32[]{:S(2)}) collective-permute-start(bf16[4,256]{1,0:T(4,128)(2,1)S(1)} %bitcast.49), channel_id=1, source_target_pairs={{0,8},{8,0},{16,24},{24,16},{1,9},{9,1},{17,25},{25,17},{2,10},{10... | collective-permute-start | bytes 6152 | tf_op jit(solution)/shard_map/ppermute | solution.py:185
  54.2 0.0 collective-permute-done.4.refs_6_
  54.2 1.6 %collective-permute-done.3.refs_5_ = bf16[4,256]{1,0:T(4,128)(2,1)S(1)} collective-permute-done((bf16[4,256]{1,0:T(4,128)(2,1)S(1)}, bf16[4,256]{1,0:T(4,128)(2,1)S(1)}, u32[]{:S(2)}, u32[]{:S(2)}) %collective-permute-start.3) | collective-permute-done | bytes 2080 | tf_op jit(solution)/shard_map/ppermute | solution.py:185
  55.8 0.0 collective-permute-done.2.refs_3_
  55.8 0.0 collective-permute-done.1.refs_2_
  55.8 0.8 copy-done.2
  56.6 0.0 collective-permute-done.refs_1_
  56.6 0.8 copy-done.4
  57.4 1.0 copy-done.3
  58.4 1.0 copy-done.5
  59.5 1.4 %shard_map.110 = (f32[4,64,1024]{2,1,0:T(8,128)S(1)}, f32[4,256]{1,0:T(4,128)S(1)}, f32[16,2,16,128]{3,2,1,0:T(8,128)}) custom-call(s32[1]{0:T(128)} %bitcast.1.section_ref, bf16[4,64,1024]{2,1,0:T(8,128)(2,1)S(1)} %get-tuple-element.38.refs_0_, bf16[4,64,1024]{2,1,0:T(8,128)(2,1)S(1)} %copy-done.5, bf16[4,64,1024]{2,1,0:T(8,128)(2,1)S(1)} %copy-done.3, ...), custom_call_target="tpu_custom_call" | custom-call | tf_op jit(solution)/shard_map/pallas_call | solution.py:174
  60.9 5.3 %all-to-all-start = ((f32[32,16,128]{2,1,0:T(8,128)}), f32[32,16,128]{2,1,0:T(8,128)S(1)}, u32[]{:S(2)}, u32[]{:S(2)}) async-start(f32[32,16,128]{2,1,0:T(8,128)} %bitcast.8), calls=%async_computation | async-start | bytes 524288 | tf_op jit(solution)/shard_map/all_to_all | solution.py:223
  66.2 10.6 %all-to-all-done.figures_ref = f32[32,16,128]{2,1,0:T(8,128)S(1)} async-done(((f32[32,16,128]{2,1,0:T(8,128)}), f32[32,16,128]{2,1,0:T(8,128)S(1)}, u32[]{:S(2)}, u32[]{:S(2)}) %all-to-all-start) | async-done | bytes 262176 | tf_op jit(solution)/shard_map/all_to_all | solution.py:223
  76.8 1.0 shard_map.111
  77.8 1.0 collective-permute-start.6
  78.8 1.0 collective-permute-start.7
  79.8 2.5 %collective-permute-start.8 = (bf16[64,1024]{1,0:T(8,128)(2,1)S(1)}, bf16[64,1024]{1,0:T(8,128)(2,1)S(1)}, u32[]{:S(2)}, u32[]{:S(2)}) collective-permute-start(bf16[64,1024]{1,0:T(8,128)(2,1)S(1)} %get-tuple-element.25), channel_id=1, source_target_pairs={{0,24},{8,16},{16,8},{24,0},{1,25},{9,17},{17,9},{25,1},{2,26},{10... | collective-permute-start | bytes 393224 | tf_op jit(solution)/shard_map/ppermute | solution.py:185
  82.3 0.9 collective-permute-start.13
  83.2 0.9 collective-permute-start.9
  84.0 0.8 collective-permute-done.6.refs_1_
  84.8 0.0 collective-permute-start.14
  84.8 6.5 %collective-permute-done.7.refs_2_ = bf16[64,1024]{1,0:T(8,128)(2,1)S(1)} collective-permute-done((bf16[64,1024]{1,0:T(8,128)(2,1)S(1)}, bf16[64,1024]{1,0:T(8,128)(2,1)S(1)}, u32[]{:S(2)}, u32[]{:S(2)}) %collective-permute-start.7) | collective-permute-done | bytes 131104 | tf_op jit(solution)/shard_map/ppermute | solution.py:185
  91.3 0.1 collective-permute-start.10
  91.3 0.0 collective-permute-done.8.refs_3_
  91.3 1.4 %collective-permute-start.15 = (bf16[64,1024]{1,0:T(8,128)(2,1)S(1)}, bf16[64,1024]{1,0:T(8,128)(2,1)S(1)}, u32[]{:S(2)}, u32[]{:S(2)}) collective-permute-start(bf16[64,1024]{1,0:T(8,128)(2,1)S(1)} %collective-permute-done.7.refs_2_), channel_id=1, source_target_pairs={{0,4},{2,6},{4,0},{6,2},{1,5},{3,7},{5,1},{7,3},{8,12},{10,14},{12... | collective-permute-start | bytes 393224 | tf_op jit(solution)/shard_map/ppermute | solution.py:185
  92.8 0.0 collective-permute-done.13.refs_8_
  92.8 1.0 collective-permute-start.11
  93.7 0.0 collective-permute-done.9.refs_4_
  93.7 1.6 %collective-permute-start.16 = (bf16[64,1024]{1,0:T(8,128)(2,1)S(1)}, bf16[64,1024]{1,0:T(8,128)(2,1)S(1)}, u32[]{:S(2)}, u32[]{:S(2)}) collective-permute-start(bf16[64,1024]{1,0:T(8,128)(2,1)S(1)} %collective-permute-done.8.refs_3_), channel_id=1, source_target_pairs={{0,4},{2,6},{4,0},{6,2},{1,5},{3,7},{5,1},{7,3},{8,12},{10,14},{12... | collective-permute-start | bytes 393224 | tf_op jit(solution)/shard_map/ppermute | solution.py:185
  95.3 0.5 slice.3
  95.8 0.0 collective-permute-done.14.refs_9_
  95.8 0.1 collective-permute-start.12
  95.9 1.4 %collective-permute-done.10.refs_5_ = bf16[64,1024]{1,0:T(8,128)(2,1)S(1)} collective-permute-done((bf16[64,1024]{1,0:T(8,128)(2,1)S(1)}, bf16[64,1024]{1,0:T(8,128)(2,1)S(1)}, u32[]{:S(2)}, u32[]{:S(2)}) %collective-permute-start.10) | collective-permute-done | bytes 131104 | tf_op jit(solution)/shard_map/ppermute | solution.py:185
  97.3 0.7 collective-permute-start.17
  98.0 0.0 collective-permute-done.15.refs_10_
  98.0 1.4 %collective-permute-start.18 = (bf16[64,1024]{1,0:T(8,128)(2,1)S(1)}, bf16[64,1024]{1,0:T(8,128)(2,1)S(1)}, u32[]{:S(2)}, u32[]{:S(2)}) collective-permute-start(bf16[64,1024]{1,0:T(8,128)(2,1)S(1)} %collective-permute-done.14.refs_9_), channel_id=1, source_target_pairs={{0,2},{2,0},{4,6},{6,4},{1,3},{3,1},{5,7},{7,5},{8,10},{10,8},{12,... | collective-permute-start | bytes 393224 | tf_op jit(solution)/shard_map/ppermute | solution.py:185
  99.4 0.7 collective-permute-done.11.refs_6_
  100.1 0.7 collective-permute-start.19
  100.8 0.0 collective-permute-done.16.refs_11_
  100.8 1.1 collective-permute-start.20
  101.9 1.9 %add_bitcast_fusion = f32[1,4,64,1024]{3,2,1,0:T(8,128)} fusion(f32[4,64,1024]{2,1,0:T(8,128)S(1)} %get-tuple-element.20.grad_ref, f32[]{:T(128)} %bitcast.9, f32[1,4,64,1024]{3,2,1,0:T(8,128)S(1)} %copy-done), kind=kLoop, calls=%fused_computation | loop fusion | flops 786432 | bytes 3145732 | tf_op jit(solution)/shard_map/broadcast_in_dim | solution.py:270
  103.8 0.0 collective-permute-done.12.refs_7_
  103.8 0.0 collective-permute-done.17.refs_12_
  103.8 0.8 collective-permute-done.18.refs_13_
  104.6 0.4 collective-permute-done.19.refs_14_
  105.1 1.0 collective-permute-done.20.refs_15_
  106.1 10.2 %shard_map.112 = (bf16[64,1024]{1,0:T(8,128)(2,1)S(1)}, bf16[64,1024]{1,0:T(8,128)(2,1)S(1)}, bf16[64,1024]{1,0:T(8,128)(2,1)S(1)}, bf16[64,1024]{1,0:T(8,128)(2,1)S(1)}) custom-call(bf16[64,1024]{1,0:T(8,128)(2,1)S(1)} %get-tuple-element.22.refs_0_, bf16[64,1024]{1,0:T(8,128)(2,1)S(1)} %collective-permute-done.6.refs_1_, ...), custom_call_target="tpu_custom_call" | custom-call | tf_op jit(solution)/shard_map/pallas_call | solution.py:84
  116.3 1.8 %collective-permute-start.21 = (bf16[64,1024]{1,0:T(8,128)(2,1)S(1)}, bf16[64,1024]{1,0:T(8,128)(2,1)S(1)}, u32[]{:S(2)}, u32[]{:S(2)}) collective-permute-start(bf16[64,1024]{1,0:T(8,128)(2,1)S(1)} %get-tuple-element.27), channel_id=1, source_target_pairs={{0,8},{8,0},{16,24},{24,16},{1,9},{9,1},{17,25},{25,17},{2,10},{10... | collective-permute-start | bytes 393224 | tf_op jit(solution)/shard_map/ppermute | solution.py:185
  118.1 0.9 collective-permute-start.22
  119.0 1.8 %collective-permute-start.23 = (bf16[64,1024]{1,0:T(8,128)(2,1)S(1)}, bf16[64,1024]{1,0:T(8,128)(2,1)S(1)}, u32[]{:S(2)}, u32[]{:S(2)}) collective-permute-start(bf16[64,1024]{1,0:T(8,128)(2,1)S(1)} %get-tuple-element.29), channel_id=1, source_target_pairs={{0,24},{8,16},{16,8},{24,0},{1,25},{9,17},{17,9},{25,1},{2,26},{10... | collective-permute-start | bytes 393224 | tf_op jit(solution)/shard_map/ppermute | solution.py:185
  120.7 1.3 %multiply_subtract_fusion = (f32[1,4,64]{2,1,0:T(4,128)}, f32[1,4,64]{2,1,0:T(4,128)}) fusion(f32[1,4,64]{2,1,0:T(4,128)S(1)} %copy-done.7, f32[1,4,64]{2,1,0:T(4,128)S(1)} %copy-done.8, f32[4,256]{1,0:T(4,128)S(1)} %get-tuple-element.32, s32[]{:T(128)S(6)} %select_n.20, f32[]{:T(128)} %bitcast.9, f32[1,4,64]{2,1,0:T(4,128)S(1)} %copy-done.9), kind=kLoop, calls=%fused_computation.12 | loop fusion | flops 3328 | bytes 6152 | tf_op jit(solution)/shard_map/sub | solution.py:268
  122.1 0.0 collective-permute-done.21.refs_1_
  122.1 7.1 %collective-permute-done.22.refs_2_ = bf16[64,1024]{1,0:T(8,128)(2,1)S(1)} collective-permute-done((bf16[64,1024]{1,0:T(8,128)(2,1)S(1)}, bf16[64,1024]{1,0:T(8,128)(2,1)S(1)}, u32[]{:S(2)}, u32[]{:S(2)}) %collective-permute-start.22) | collective-permute-done | bytes 131104 | tf_op jit(solution)/shard_map/ppermute | solution.py:185
  129.2 0.0 collective-permute-done.23.refs_3_
  129.2 1.6 %shard_map.113 = (bf16[4,64,1024]{2,1,0:T(8,128)(2,1)}, bf16[4,64,1024]{2,1,0:T(8,128)(2,1)}) custom-call(s32[4]{0:T(128)S(1)} %iota_xor_fusion.order_ref, bf16[64,1024]{1,0:T(8,128)(2,1)S(1)} %get-tuple-element.26.refs_0_, bf16[64,1024]{1,0:T(8,128)(2,1)S(1)} %collective-permute-done.21.refs_1_, bf16[64,1024]{1,0:T(8,128)(2,1)S(1)} %collective-permute-done.22.refs_2_, ...), custom_call_target="tpu_custom_call" | custom-call | tf_op jit(solution)/shard_map/pallas_call | solution.py:174
  (15 shorter events, 0.0 us)
Async XLA Ops:
  0.7 8.4 %copy-start.6 = (bf16[1,1,4,256]{3,2,1,0:T(4,128)(2,1)S(1)}, bf16[1,1,4,256]{3,2,1,0:T(4,128)(2,1)}, u32[]{:S(2)}) copy-start(bf16[1,1,4,256]{3,2,1,0:T(4,128)(2,1)} %param.8) | copy-start | bytes 6148
  0.7 56.7 %copy-start = (f32[1,4,64,1024]{3,2,1,0:T(8,128)S(1)}, f32[1,4,64,1024]{3,2,1,0:T(8,128)}, u32[]{:S(2)}) copy-start(f32[1,4,64,1024]{3,2,1,0:T(8,128)} %param.9) | copy-start | bytes 3145732
  3.5 52.3 %collective-permute-start.2 = (bf16[4,64,1024]{2,1,0:T(8,128)(2,1)}, bf16[4,64,1024]{2,1,0:T(8,128)(2,1)S(1)}, u32[]{:S(2)}, u32[]{:S(2)}) collective-permute-start(bf16[4,64,1024]{2,1,0:T(8,128)(2,1)} %get-tuple-element.35), channel_id=1, source_target_pairs={{0,24},{8,16},{16,8},{24,0},{1,25},{9,17},{17,9},{25,1},{2,26},{10... | collective-permute-start | bytes 1572872 | tf_op jit(solution)/shard_map/ppermute | solution.py:185
  8.5 47.3 %collective-permute-start.1 = (bf16[4,64,1024]{2,1,0:T(8,128)(2,1)}, bf16[4,64,1024]{2,1,0:T(8,128)(2,1)S(1)}, u32[]{:S(2)}, u32[]{:S(2)}) collective-permute-start(bf16[4,64,1024]{2,1,0:T(8,128)(2,1)} %get-tuple-element.36), channel_id=1, source_target_pairs={{0,16},{8,24},{16,0},{24,8},{1,17},{9,25},{17,1},{25,9},{2,18},{10... | collective-permute-start | bytes 1572872 | tf_op jit(solution)/shard_map/ppermute | solution.py:185
  8.5 48.1 %collective-permute-start = (bf16[4,64,1024]{2,1,0:T(8,128)(2,1)}, bf16[4,64,1024]{2,1,0:T(8,128)(2,1)S(1)}, u32[]{:S(2)}, u32[]{:S(2)}) collective-permute-start(bf16[4,64,1024]{2,1,0:T(8,128)(2,1)} %get-tuple-element.37), channel_id=1, source_target_pairs={{0,8},{8,0},{16,24},{24,16},{1,9},{9,1},{17,25},{25,17},{2,10},{10... | collective-permute-start | bytes 1572872 | tf_op jit(solution)/shard_map/ppermute | solution.py:185
  9.1 34.3 %collective-permute-start.5 = (bf16[4,256]{1,0:T(4,128)(2,1)S(1)}, bf16[4,256]{1,0:T(4,128)(2,1)S(1)}, u32[]{:S(2)}, u32[]{:S(2)}) collective-permute-start(bf16[4,256]{1,0:T(4,128)(2,1)S(1)} %bitcast.47), channel_id=1, source_target_pairs={{0,24},{8,16},{16,8},{24,0},{1,25},{9,17},{17,9},{25,1},{2,26},{10... | collective-permute-start | bytes 6152 | tf_op jit(solution)/shard_map/ppermute | solution.py:185
  12.9 41.3 %collective-permute-start.4 = (bf16[4,256]{1,0:T(4,128)(2,1)S(1)}, bf16[4,256]{1,0:T(4,128)(2,1)S(1)}, u32[]{:S(2)}, u32[]{:S(2)}) collective-permute-start(bf16[4,256]{1,0:T(4,128)(2,1)S(1)} %bitcast.48), channel_id=1, source_target_pairs={{0,16},{8,24},{16,0},{24,8},{1,17},{9,25},{17,1},{25,9},{2,18},{10... | collective-permute-start | bytes 6152 | tf_op jit(solution)/shard_map/ppermute | solution.py:185
  43.4 12.4 %collective-permute-start.3 = (bf16[4,256]{1,0:T(4,128)(2,1)S(1)}, bf16[4,256]{1,0:T(4,128)(2,1)S(1)}, u32[]{:S(2)}, u32[]{:S(2)}) collective-permute-start(bf16[4,256]{1,0:T(4,128)(2,1)S(1)} %bitcast.49), channel_id=1, source_target_pairs={{0,8},{8,0},{16,24},{24,16},{1,9},{9,1},{17,25},{25,17},{2,10},{10... | collective-permute-start | bytes 6152 | tf_op jit(solution)/shard_map/ppermute | solution.py:185
  55.8 0.8 copy-start.2
  56.6 0.8 copy-start.4
  57.4 1.0 copy-start.3
  58.4 1.0 copy-start.5
  60.9 15.9 %all-to-all-start = ((f32[32,16,128]{2,1,0:T(8,128)}), f32[32,16,128]{2,1,0:T(8,128)S(1)}, u32[]{:S(2)}, u32[]{:S(2)}) async-start(f32[32,16,128]{2,1,0:T(8,128)} %bitcast.8), calls=%async_computation | async-start | bytes 524288 | tf_op jit(solution)/shard_map/all_to_all | solution.py:223
  77.8 7.0 %collective-permute-start.6 = (bf16[64,1024]{1,0:T(8,128)(2,1)S(1)}, bf16[64,1024]{1,0:T(8,128)(2,1)S(1)}, u32[]{:S(2)}, u32[]{:S(2)}) collective-permute-start(bf16[64,1024]{1,0:T(8,128)(2,1)S(1)} %get-tuple-element.23), channel_id=1, source_target_pairs={{0,8},{8,0},{16,24},{24,16},{1,9},{9,1},{17,25},{25,17},{2,10},{10... | collective-permute-start | bytes 393224 | tf_op jit(solution)/shard_map/ppermute | solution.py:185
  78.8 12.4 %collective-permute-start.7 = (bf16[64,1024]{1,0:T(8,128)(2,1)S(1)}, bf16[64,1024]{1,0:T(8,128)(2,1)S(1)}, u32[]{:S(2)}, u32[]{:S(2)}) collective-permute-start(bf16[64,1024]{1,0:T(8,128)(2,1)S(1)} %get-tuple-element.24), channel_id=1, source_target_pairs={{0,16},{8,24},{16,0},{24,8},{1,17},{9,25},{17,1},{25,9},{2,18},{10... | collective-permute-start | bytes 393224 | tf_op jit(solution)/shard_map/ppermute | solution.py:185
  79.8 11.5 %collective-permute-start.8 = (bf16[64,1024]{1,0:T(8,128)(2,1)S(1)}, bf16[64,1024]{1,0:T(8,128)(2,1)S(1)}, u32[]{:S(2)}, u32[]{:S(2)}) collective-permute-start(bf16[64,1024]{1,0:T(8,128)(2,1)S(1)} %get-tuple-element.25), channel_id=1, source_target_pairs={{0,24},{8,16},{16,8},{24,0},{1,25},{9,17},{17,9},{25,1},{2,26},{10... | collective-permute-start | bytes 393224 | tf_op jit(solution)/shard_map/ppermute | solution.py:185
  82.3 10.5 %collective-permute-start.13 = (bf16[64,1024]{1,0:T(8,128)(2,1)S(1)}, bf16[64,1024]{1,0:T(8,128)(2,1)S(1)}, u32[]{:S(2)}, u32[]{:S(2)}) collective-permute-start(bf16[64,1024]{1,0:T(8,128)(2,1)S(1)} %get-tuple-element.22.refs_0_), channel_id=1, source_target_pairs={{0,4},{2,6},{4,0},{6,2},{1,5},{3,7},{5,1},{7,3},{8,12},{10,14},{12... | collective-permute-start | bytes 393224 | tf_op jit(solution)/shard_map/ppermute | solution.py:185
  83.2 10.6 %collective-permute-start.9 = (bf16[64,1024]{1,0:T(8,128)(2,1)S(1)}, bf16[64,1024]{1,0:T(8,128)(2,1)S(1)}, u32[]{:S(2)}, u32[]{:S(2)}) collective-permute-start(bf16[64,1024]{1,0:T(8,128)(2,1)S(1)} %get-tuple-element.22.refs_0_), channel_id=1, source_target_pairs={{0,2},{2,0},{4,6},{6,4},{1,3},{3,1},{5,7},{7,5},{8,10},{10,8},{12,... | collective-permute-start | bytes 393224 | tf_op jit(solution)/shard_map/ppermute | solution.py:185
  84.8 11.0 %collective-permute-start.14 = (bf16[64,1024]{1,0:T(8,128)(2,1)S(1)}, bf16[64,1024]{1,0:T(8,128)(2,1)S(1)}, u32[]{:S(2)}, u32[]{:S(2)}) collective-permute-start(bf16[64,1024]{1,0:T(8,128)(2,1)S(1)} %collective-permute-done.6.refs_1_), channel_id=1, source_target_pairs={{0,4},{2,6},{4,0},{6,2},{1,5},{3,7},{5,1},{7,3},{8,12},{10,14},{12... | collective-permute-start | bytes 393224 | tf_op jit(solution)/shard_map/ppermute | solution.py:185
  91.3 6.0 %collective-permute-start.10 = (bf16[64,1024]{1,0:T(8,128)(2,1)S(1)}, bf16[64,1024]{1,0:T(8,128)(2,1)S(1)}, u32[]{:S(2)}, u32[]{:S(2)}) collective-permute-start(bf16[64,1024]{1,0:T(8,128)(2,1)S(1)} %collective-permute-done.6.refs_1_), channel_id=1, source_target_pairs={{0,2},{2,0},{4,6},{6,4},{1,3},{3,1},{5,7},{7,5},{8,10},{10,8},{12,... | collective-permute-start | bytes 393224 | tf_op jit(solution)/shard_map/ppermute | solution.py:185
  91.3 6.7 %collective-permute-start.15 = (bf16[64,1024]{1,0:T(8,128)(2,1)S(1)}, bf16[64,1024]{1,0:T(8,128)(2,1)S(1)}, u32[]{:S(2)}, u32[]{:S(2)}) collective-permute-start(bf16[64,1024]{1,0:T(8,128)(2,1)S(1)} %collective-permute-done.7.refs_2_), channel_id=1, source_target_pairs={{0,4},{2,6},{4,0},{6,2},{1,5},{3,7},{5,1},{7,3},{8,12},{10,14},{12... | collective-permute-start | bytes 393224 | tf_op jit(solution)/shard_map/ppermute | solution.py:185
  92.8 7.3 %collective-permute-start.11 = (bf16[64,1024]{1,0:T(8,128)(2,1)S(1)}, bf16[64,1024]{1,0:T(8,128)(2,1)S(1)}, u32[]{:S(2)}, u32[]{:S(2)}) collective-permute-start(bf16[64,1024]{1,0:T(8,128)(2,1)S(1)} %collective-permute-done.7.refs_2_), channel_id=1, source_target_pairs={{0,2},{2,0},{4,6},{6,4},{1,3},{3,1},{5,7},{7,5},{8,10},{10,8},{12,... | collective-permute-start | bytes 393224 | tf_op jit(solution)/shard_map/ppermute | solution.py:185
  93.7 7.1 %collective-permute-start.16 = (bf16[64,1024]{1,0:T(8,128)(2,1)S(1)}, bf16[64,1024]{1,0:T(8,128)(2,1)S(1)}, u32[]{:S(2)}, u32[]{:S(2)}) collective-permute-start(bf16[64,1024]{1,0:T(8,128)(2,1)S(1)} %collective-permute-done.8.refs_3_), channel_id=1, source_target_pairs={{0,4},{2,6},{4,0},{6,2},{1,5},{3,7},{5,1},{7,3},{8,12},{10,14},{12... | collective-permute-start | bytes 393224 | tf_op jit(solution)/shard_map/ppermute | solution.py:185
  95.8 8.0 %collective-permute-start.12 = (bf16[64,1024]{1,0:T(8,128)(2,1)S(1)}, bf16[64,1024]{1,0:T(8,128)(2,1)S(1)}, u32[]{:S(2)}, u32[]{:S(2)}) collective-permute-start(bf16[64,1024]{1,0:T(8,128)(2,1)S(1)} %collective-permute-done.8.refs_3_), channel_id=1, source_target_pairs={{0,2},{2,0},{4,6},{6,4},{1,3},{3,1},{5,7},{7,5},{8,10},{10,8},{12,... | collective-permute-start | bytes 393224 | tf_op jit(solution)/shard_map/ppermute | solution.py:185
  97.3 6.5 %collective-permute-start.17 = (bf16[64,1024]{1,0:T(8,128)(2,1)S(1)}, bf16[64,1024]{1,0:T(8,128)(2,1)S(1)}, u32[]{:S(2)}, u32[]{:S(2)}) collective-permute-start(bf16[64,1024]{1,0:T(8,128)(2,1)S(1)} %collective-permute-done.9.refs_4_), channel_id=1, source_target_pairs={{0,4},{2,6},{4,0},{6,2},{1,5},{3,7},{5,1},{7,3},{8,12},{10,14},{12... | collective-permute-start | bytes 393224 | tf_op jit(solution)/shard_map/ppermute | solution.py:185
  98.0 6.7 %collective-permute-start.18 = (bf16[64,1024]{1,0:T(8,128)(2,1)S(1)}, bf16[64,1024]{1,0:T(8,128)(2,1)S(1)}, u32[]{:S(2)}, u32[]{:S(2)}) collective-permute-start(bf16[64,1024]{1,0:T(8,128)(2,1)S(1)} %collective-permute-done.14.refs_9_), channel_id=1, source_target_pairs={{0,2},{2,0},{4,6},{6,4},{1,3},{3,1},{5,7},{7,5},{8,10},{10,8},{12,... | collective-permute-start | bytes 393224 | tf_op jit(solution)/shard_map/ppermute | solution.py:185
  100.1 5.0 %collective-permute-start.19 = (bf16[64,1024]{1,0:T(8,128)(2,1)S(1)}, bf16[64,1024]{1,0:T(8,128)(2,1)S(1)}, u32[]{:S(2)}, u32[]{:S(2)}) collective-permute-start(bf16[64,1024]{1,0:T(8,128)(2,1)S(1)} %collective-permute-done.11.refs_6_), channel_id=1, source_target_pairs={{0,4},{2,6},{4,0},{6,2},{1,5},{3,7},{5,1},{7,3},{8,12},{10,14},{12... | collective-permute-start | bytes 393224 | tf_op jit(solution)/shard_map/ppermute | solution.py:185
  100.8 5.3 %collective-permute-start.20 = (bf16[64,1024]{1,0:T(8,128)(2,1)S(1)}, bf16[64,1024]{1,0:T(8,128)(2,1)S(1)}, u32[]{:S(2)}, u32[]{:S(2)}) collective-permute-start(bf16[64,1024]{1,0:T(8,128)(2,1)S(1)} %collective-permute-done.16.refs_11_), channel_id=1, source_target_pairs={{0,2},{2,0},{4,6},{6,4},{1,3},{3,1},{5,7},{7,5},{8,10},{10,8},{12,... | collective-permute-start | bytes 393224 | tf_op jit(solution)/shard_map/ppermute | solution.py:185
  101.9 18.8 %copy-start.7 = (f32[1,4,64]{2,1,0:T(4,128)S(1)}, f32[1,4,64]{2,1,0:T(4,128)}, u32[]{:S(2)}) copy-start(f32[1,4,64]{2,1,0:T(4,128)} %param.11) | copy-start | bytes 3076
  101.9 18.8 %copy-start.8 = (f32[1,4,64]{2,1,0:T(4,128)S(1)}, f32[1,4,64]{2,1,0:T(4,128)}, u32[]{:S(2)}) copy-start(f32[1,4,64]{2,1,0:T(4,128)} %param.13) | copy-start | bytes 3076
  101.9 18.8 %copy-start.9 = (f32[1,4,64]{2,1,0:T(4,128)S(1)}, f32[1,4,64]{2,1,0:T(4,128)}, u32[]{:S(2)}) copy-start(f32[1,4,64]{2,1,0:T(4,128)} %param.12) | copy-start | bytes 3076
  101.9 27.2 %copy-start.1 = (bf16[1,4,64,1024]{3,2,1,0:T(8,128)(2,1)S(1)}, bf16[1,4,64,1024]{3,2,1,0:T(8,128)(2,1)}, u32[]{:S(2)}) copy-start(bf16[1,4,64,1024]{3,2,1,0:T(8,128)(2,1)} %param.10) | copy-start | bytes 1572868
  116.3 5.8 %collective-permute-start.21 = (bf16[64,1024]{1,0:T(8,128)(2,1)S(1)}, bf16[64,1024]{1,0:T(8,128)(2,1)S(1)}, u32[]{:S(2)}, u32[]{:S(2)}) collective-permute-start(bf16[64,1024]{1,0:T(8,128)(2,1)S(1)} %get-tuple-element.27), channel_id=1, source_target_pairs={{0,8},{8,0},{16,24},{24,16},{1,9},{9,1},{17,25},{25,17},{2,10},{10... | collective-permute-start | bytes 393224 | tf_op jit(solution)/shard_map/ppermute | solution.py:185
  118.1 11.1 %collective-permute-start.22 = (bf16[64,1024]{1,0:T(8,128)(2,1)S(1)}, bf16[64,1024]{1,0:T(8,128)(2,1)S(1)}, u32[]{:S(2)}, u32[]{:S(2)}) collective-permute-start(bf16[64,1024]{1,0:T(8,128)(2,1)S(1)} %get-tuple-element.28), channel_id=1, source_target_pairs={{0,16},{8,24},{16,0},{24,8},{1,17},{9,25},{17,1},{25,9},{2,18},{10... | collective-permute-start | bytes 393224 | tf_op jit(solution)/shard_map/ppermute | solution.py:185
  119.0 10.2 %collective-permute-start.23 = (bf16[64,1024]{1,0:T(8,128)(2,1)S(1)}, bf16[64,1024]{1,0:T(8,128)(2,1)S(1)}, u32[]{:S(2)}, u32[]{:S(2)}) collective-permute-start(bf16[64,1024]{1,0:T(8,128)(2,1)S(1)} %get-tuple-element.29), channel_id=1, source_target_pairs={{0,24},{8,16},{16,8},{24,0},{1,25},{9,17},{17,9},{25,1},{2,26},{10... | collective-permute-start | bytes 393224 | tf_op jit(solution)/shard_map/ppermute | solution.py:185
where the time goes:
time: 131 us
  waiting for transfers between devices  61.3 us (47%)
  starting transfers between devices  44.3 us (34%)
  Pallas kernels  14.3 us (11%)
  local copies, waits for them, and re-layouts  6.99 us (5%)
  other arithmetic  3.19 us (2%)
    ppermute x24, waiting for transfers between devices, swapped(): return lax.ppermute(array, axis, pairs)  50.7 us
    ppermute x24, starting transfers between devices, swapped(): return lax.ppermute(array, axis, pairs)  39 us
    all_to_all x1, waiting for transfers between devices, per_device(): lax.all_to_all(figures.reshape(others * section_count, FIGURES, LANES), M...  10.6 us
    pallas_call x1, Pallas kernels, orthogonalize(): pl.pallas_call(functools.partial(orthogonalize_kernel, count, pieces), ou...  10.2 us
    all_to_all x1, starting transfers between devices, per_device(): lax.all_to_all(figures.reshape(others * section_count, FIGURES, LANES), M...  5.28 us
    pallas_call x3, Pallas kernels, on_device(): pl.pallas_call(kernel, out_shape=out_shape, in_specs=[pl.BlockSpec(memory...  4.09 us
    unnamed x20, local copies, waits for them, and re-layouts  3.69 us
    squeeze x1, local copies, waits for them, and re-layouts, per_device(): lax.dynamic_index_in_dim(by_rows, shard_index ^ offset, 1, keepdims=False)  2.79 us
  transfers between devices with their start and end apart: 25, of which 11 were waited for; matrix products, arithmetic and copies ran while one was open for 3% of the time, Pallas kernels for 0%

commit v1 on v0

--- a/solution.py
+++ b/solution.py
@@ -24,6 +24,7 @@
 
 VECTOR_ROWS = 16
 FIGURES = 16
+MIB = 2**20
 LANES = 128
 MESH_AXES = ("shard", "tensor", "section")
 
@@ -89,7 +90,7 @@
             pltpu.VMEM((count, pieces * height, width), jnp.bfloat16),
             pltpu.VMEM((count, pieces * height, width), jnp.bfloat16),
         ],
-        compiler_params=pltpu.CompilerParams(vmem_limit_bytes=48 * 2**20),
+        compiler_params=pltpu.CompilerParams(vmem_limit_bytes=24 * MIB),
     )(*[piece for block in blocks for piece in block])
 
 
@@ -124,18 +125,25 @@
     lines = squares + crosses + momentum_squares + [total]
     lines = lines + [jnp.zeros_like(total)] * (FIGURES - len(lines))
     tile = jnp.concatenate(lines, axis=0)
+    sums = jnp.sum(tile, axis=1, keepdims=True)
     line_index = lax.broadcasted_iota(jnp.int32, tile.shape, 0)
-    total_only = jnp.where(line_index == 3 * momentum_ref.shape[0], tile, 0.0)
+    lane_index = lax.broadcasted_iota(jnp.int32, tile.shape, 1)
+    line = jnp.sum(jnp.where(line_index == lane_index, sums, 0.0), axis=0, keepdims=True)
+    total_only = jnp.where(lane_index[:1] == 3 * momentum_ref.shape[0], line, 0.0)
     for section in range(figures_ref.shape[1]):
-        chosen = jnp.where(section_ref[0] == section, tile, total_only)
+        chosen = jnp.where(section_ref[0] == section, line, total_only)
         figures_ref[:, section] = jnp.broadcast_to(
-            chosen[None], (figures_ref.shape[0],) + tile.shape
+            chosen[None], (figures_ref.shape[0],) + line.shape
         )
 
 
 def scale_kernel(matrix_count, order_ref, figures_ref, grad_ref, momentum_ref, *refs):
-    outputs, clip_ref = refs[:matrix_count], refs[matrix_count]
-    sums = jnp.sum(jnp.sum(figures_ref[...], axis=0), axis=1, keepdims=True)
+    outputs = refs[:matrix_count]
+    clip_ref, new_momentum_ref = refs[matrix_count:]
+    line = jnp.sum(figures_ref[...], axis=0)
+    line_index = lax.broadcasted_iota(jnp.int32, (FIGURES, LANES), 0)
+    lane_index = lax.broadcasted_iota(jnp.int32, (FIGURES, LANES), 1)
+    sums = jnp.sum(jnp.where(line_index == lane_index, line, 0.0), axis=1, keepdims=True)
     total = sums[3 * matrix_count : 3 * matrix_count + 1]
     clip = jnp.minimum(1.0, max_norm / (jnp.sqrt(total) + 1e-06))
     clip_ref[...] = jnp.broadcast_to(clip, clip_ref.shape)
@@ -152,7 +160,9 @@
         matrix = order_ref[place]
         factor = jnp.sum(jnp.where(position == matrix, inverse, 0.0), axis=0, keepdims=True)
         clipped = clip * grad_ref[matrix]
-        nesterov = clipped + mom_beta * (mom_beta * momentum_ref[matrix] + clipped)
+        new_momentum = mom_beta * momentum_ref[matrix] + clipped
+        new_momentum_ref[matrix] = new_momentum
+        nesterov = clipped + mom_beta * new_momentum
         outputs[place][...] = (nesterov * factor).astype(jnp.bfloat16)
 
 
@@ -176,13 +186,17 @@
         out_shape=out_shape,
         in_specs=[pl.BlockSpec(memory_space=pltpu.SMEM)]
         + [pl.BlockSpec(memory_space=pltpu.VMEM)] * len(operands),
-        compiler_params=pltpu.CompilerParams(vmem_limit_bytes=32 * 2**20),
+        compiler_params=pltpu.CompilerParams(vmem_limit_bytes=12 * MIB),
     )(scalars, *operands)
 
 
 def swapped(array, axis, offset):
     pairs = [(i, i ^ offset) for i in range(lax.axis_size(axis))]
     return lax.ppermute(array, axis, pairs)
+
+
+def after(array, earlier):
+    return lax.optimization_barrier((array, earlier))[0]
 
 
 def per_device(grad_parts, vector_grads, momentum, weights, vectors, first_moment, second_moment):
@@ -201,13 +215,15 @@
 
     by_rows = grad_parts.reshape(matrix_count, shard_count, local_height, width)
     own_vectors = vector_grads.reshape(vector_count, shard_count * vector_width)
+    vector_parts = [own_vectors] + [
+        swapped(own_vectors, "shard", offset) for offset in range(1, shard_count)
+    ]
     parts = [None] * shard_count
-    vector_parts = [own_vectors] + [None] * (shard_count - 1)
+    index = shard_index
     for offset in reversed(range(shard_count)):
-        rows = lax.dynamic_index_in_dim(by_rows, shard_index ^ offset, 1, keepdims=False)
+        rows = lax.dynamic_index_in_dim(by_rows, index ^ offset, 1, keepdims=False)
+        index, rows, vector_parts = lax.optimization_barrier((index, rows, vector_parts))
         parts[offset] = swapped(rows, "shard", offset) if offset else rows
-    for offset in range(1, shard_count):
-        vector_parts[offset] = swapped(own_vectors, "shard", offset)
 
     others = shard_count * tensor_count
     grad_rows, vector_whole, figures = on_device(
@@ -217,33 +233,44 @@
         [
             jax.ShapeDtypeStruct(own_momentum.shape, jnp.float32),
             jax.ShapeDtypeStruct(own_vectors.shape, jnp.float32),
-            jax.ShapeDtypeStruct((others, section_count, FIGURES, LANES), jnp.float32),
+            jax.ShapeDtypeStruct((others, section_count, 1, LANES), jnp.float32),
         ],
     )
     figures = lax.all_to_all(
-        figures.reshape(others * section_count, FIGURES, LANES),
+        figures.reshape(others * section_count, 1, LANES),
         MESH_AXES,
         split_axis=0,
         concat_axis=0,
         tiled=True,
     )
-    *scaled, clip_tile = on_device(
+    *scaled, clip_tile, new_momentum = on_device(
         functools.partial(scale_kernel, matrix_count),
         order,
         [figures, grad_rows, own_momentum],
         [jax.ShapeDtypeStruct((local_height, width), jnp.bfloat16)] * matrix_count
-        + [jax.ShapeDtypeStruct((8, LANES), jnp.float32)],
-    )
-
-    blocks = [[], [], [], []]
-    for offset in range(shard_count):
-        piece = swapped(scaled[offset], "shard", offset) if offset else scaled[0]
-        near = swapped(piece, "tensor", 1)
-        side = swapped(piece, "tensor", 2)
-        far = swapped(near, "tensor", 2) if offset % 2 == 0 else swapped(side, "tensor", 1)
-        for block, held in zip(blocks, (piece, near, side, far)):
-            block.append(held)
-    results = orthogonalize(blocks)
+        + [
+            jax.ShapeDtypeStruct((8, LANES), jnp.float32),
+            jax.ShapeDtypeStruct(own_momentum.shape, jnp.float32),
+        ],
+    )
+
+    pieces = [scaled[0]] + [None] * 3
+    for offset in (2, 3, 1):
+        pieces[offset] = swapped(scaled[offset], "shard", offset)
+    near, side, far = [None] * 4, [None] * 4, [None] * 4
+    near[0] = swapped(pieces[0], "tensor", 1)
+    side[0] = swapped(pieces[0], "tensor", 2)
+    far[0] = swapped(near[0], "tensor", 2)
+    near[1] = swapped(pieces[1], "tensor", 1)
+    side[1] = swapped(after(pieces[1], side[0]), "tensor", 2)
+    far[1] = swapped(side[1], "tensor", 1)
+    near[2] = swapped(after(pieces[2], far[0]), "tensor", 1)
+    side[2] = swapped(after(pieces[2], near[1]), "tensor", 2)
+    far[2] = swapped(near[2], "tensor", 2)
+    near[3] = swapped(after(pieces[3], far[1]), "tensor", 1)
+    side[3] = swapped(after(pieces[3], side[2]), "tensor", 2)
+    far[3] = swapped(side[3], "tensor", 1)
+    results = orthogonalize([pieces, near, side, far])
 
     arrived = [
         swapped(results[offset], "shard", offset) if offset else results[0]
@@ -256,8 +283,7 @@
         [jax.ShapeDtypeStruct(own_momentum.shape, jnp.bfloat16)] * 2,
     )
 
-    clip_factor = clip_tile[0, 0]
-    new_momentum = mom_beta * own_momentum + clip_factor * grad_rows
+    clip_factor = after(clip_tile, results[0])[0, 0]
     vector_rows = lax.dynamic_slice_in_dim(
         vector_whole, shard_index * vector_width, vector_width, 1
     )

time: 131 us -> 135 us (1.031)
  local copies, waits for them, and re-layouts: 6.99 us -> 11.5 us
  starting transfers between devices: 44.3 us -> 40.3 us
  Pallas kernels: 14.3 us -> 17.7 us
    ppermute x24, starting transfers between devices: 39 us -> 27.4 us  [swapped(): return lax.ppermute(array, axis, pairs)]
    all_to_all x1, starting transfers between devices: 5.28 us -> 12.9 us  [per_device(): lax.all_to_all(figures.reshape(others * section_count, 1, LANES), MESH_AX...]
    unnamed x20 -> x30, local copies, waits for them, and re-layouts: 3.69 us -> 8.42 us
    ppermute x24, waiting for transfers between devices: 50.7 us -> 55.4 us  [swapped(): return lax.ppermute(array, axis, pairs)]
    all_to_all x1, waiting for transfers between devices: 10.6 us -> 7.06 us  [per_device(): lax.all_to_all(figures.reshape(others * section_count, 1, LANES), MESH_AX...]
    pallas_call x3, Pallas kernels: 4.09 us -> 6.37 us  [on_device(): pl.pallas_call(kernel, out_shape=out_shape, in_specs=[pl.BlockSpec(memory...]
    broadcast_in_dim x1 -> x0, other arithmetic: 1.86 us -> none  [per_device(): new_momentum[None]]
    squeeze x1 -> x4, local copies, waits for them, and re-layouts: 2.79 us -> 2.52 us  [per_device(): rows = lax.dynamic_index_in_dim(by_rows, index ^ offset, 1, keepdims=False)]
  transfers between devices with their start and end apart: 25 -> 25, of which waited for: 11 -> 14; matrix products, arithmetic and copies ran while one was open for 3% -> 2% of each run, Pallas kernels for 0% -> 0%
where the time goes in v1:
time: 135 us
  waiting for transfers between devices  62.4 us (46%)
  starting transfers between devices  40.3 us (30%)
  Pallas kernels  17.7 us (13%)
  local copies, waits for them, and re-layouts  11.5 us (9%)
  other arithmetic  2.02 us (1%)
    ppermute x24, waiting for transfers between devices, swapped(): return lax.ppermute(array, axis, pairs)  55.4 us
    ppermute x24, starting transfers between devices, swapped(): return lax.ppermute(array, axis, pairs)  27.4 us
    all_to_all x1, starting transfers between devices, per_device(): lax.all_to_all(figures.reshape(others * section_count, 1, LANES), MESH_AX...  12.9 us
    pallas_call x1, Pallas kernels, orthogonalize(): pl.pallas_call(functools.partial(orthogonalize_kernel, count, pieces), ou...  11.3 us
    unnamed x30, local copies, waits for them, and re-layouts  8.42 us
    all_to_all x1, waiting for transfers between devices, per_device(): lax.all_to_all(figures.reshape(others * section_count, 1, LANES), MESH_AX...  7.06 us
    pallas_call x3, Pallas kernels, on_device(): pl.pallas_call(kernel, out_shape=out_shape, in_specs=[pl.BlockSpec(memory...  6.37 us
  transfers between devices with their start and end apart: 25, of which 14 were waited for; matrix products, arithmetic and copies ran while one was open for 2% of the time, Pallas kernels for 0%

profile of v1, /device:TPU:0, one launch (start us, length us, event | category | flops | bytes accessed | tf_op | source)
XLA Modules:
  0.0 134.6 jit_solution(9788788512656927746)
XLA Ops:
  0.6 0.0 copy-start
  0.6 5.1 %collective-permute-start.2 = (bf16[4,256]{1,0:T(4,128)(2,1)}, bf16[4,256]{1,0:T(4,128)(2,1)S(1)}, u32[]{:S(2)}, u32[]{:S(2)}) collective-permute-start(bf16[4,256]{1,0:T(4,128)(2,1)} %bitcast.49), channel_id=1, source_target_pairs={{0,24},{8,16},{16,8},{24,0},{1,25},{9,17},{17,9},{25,1},{2,26},{10... | collective-permute-start | bytes 6152 | tf_op jit(solution)/shard_map/ppermute | solution.py:195
  5.8 0.0 collective-permute-start.1
  5.8 0.6 collective-permute-start
  6.4 0.8 dynamic-slice_bitcast_fusion.3
  7.2 0.3 collective-permute-done.2.refs_7_
  7.5 2.9 %collective-permute-done.1.refs_6_ = bf16[4,256]{1,0:T(4,128)(2,1)S(1)} collective-permute-done((bf16[4,256]{1,0:T(4,128)(2,1)}, bf16[4,256]{1,0:T(4,128)(2,1)S(1)}, u32[]{:S(2)}, u32[]{:S(2)}) %collective-permute-start.1) | collective-permute-done | bytes 2080 | tf_op jit(solution)/shard_map/ppermute | solution.py:195
  10.5 0.0 collective-permute-done.refs_5_
  10.5 0.8 dynamic-slice_bitcast_fusion.2
  11.3 0.8 dynamic-slice_bitcast_fusion.1
  12.1 0.0 collective-permute-start.3
  12.1 2.1 %collective-permute-start.4 = (bf16[4,64,1024]{2,1,0:T(8,128)(2,1)}, bf16[4,64,1024]{2,1,0:T(8,128)(2,1)}, u32[]{:S(2)}, u32[]{:S(2)}) collective-permute-start(bf16[4,64,1024]{2,1,0:T(8,128)(2,1)} %dynamic-slice_bitcast_fusion.2), channel_id=1, source_target_pairs={{0,16},{8,24},{16,0},{24,8},{1,17},{9,25},{17,1},{25,9},{2,18},{10... | collective-permute-start | bytes 1572872 | tf_op jit(solution)/shard_map/ppermute | solution.py:195
  14.2 2.3 %collective-permute-start.5 = (bf16[4,64,1024]{2,1,0:T(8,128)(2,1)}, bf16[4,64,1024]{2,1,0:T(8,128)(2,1)}, u32[]{:S(2)}, u32[]{:S(2)}) collective-permute-start(bf16[4,64,1024]{2,1,0:T(8,128)(2,1)} %dynamic-slice_bitcast_fusion.3), channel_id=1, source_target_pairs={{0,24},{8,16},{16,8},{24,0},{1,25},{9,17},{17,9},{25,1},{2,26},{10... | collective-permute-start | bytes 1572872 | tf_op jit(solution)/shard_map/ppermute | solution.py:195
  16.5 18.7 %collective-permute-done.3.refs_1_ = bf16[4,64,1024]{2,1,0:T(8,128)(2,1)} collective-permute-done((bf16[4,64,1024]{2,1,0:T(8,128)(2,1)}, bf16[4,64,1024]{2,1,0:T(8,128)(2,1)}, u32[]{:S(2)}, u32[]{:S(2)}) %collective-permute-start.3) | collective-permute-done | bytes 524320 | tf_op jit(solution)/shard_map/ppermute | solution.py:195
  35.3 15.4 %collective-permute-done.4.refs_2_ = bf16[4,64,1024]{2,1,0:T(8,128)(2,1)} collective-permute-done((bf16[4,64,1024]{2,1,0:T(8,128)(2,1)}, bf16[4,64,1024]{2,1,0:T(8,128)(2,1)}, u32[]{:S(2)}, u32[]{:S(2)}) %collective-permute-start.4) | collective-permute-done | bytes 524320 | tf_op jit(solution)/shard_map/ppermute | solution.py:195
  50.7 2.8 %shard_map.110 = (f32[4,64,1024]{2,1,0:T(8,128)S(1)}, f32[4,256]{1,0:T(4,128)S(1)}, f32[16,2,1,128]{3,2,1,0:T(1,128)}) custom-call(s32[1]{0:T(128)} %bitcast.section_ref, bf16[4,64,1024]{2,1,0:T(8,128)(2,1)S(1)} %dynamic-slice_bitcast_fusion.refs_0_, bf16[4,64,1024]{2,1,0:T(8,128)(2,1)} %collective-permute-done.3.refs_1_, ...), custom_call_target="tpu_custom_call" | custom-call | tf_op jit(solution)/shard_map/pallas_call | solution.py:184
  53.4 1.0 copy-done.2
  54.4 12.9 %all-to-all-start = ((f32[32,1,128]{2,1,0:T(1,128)}), f32[32,1,128]{2,1,0:T(1,128)S(1)}, u32[]{:S(2)}, u32[]{:S(2)}) async-start(f32[32,1,128]{2,1,0:T(1,128)} %bitcast.8), calls=%async_computation | async-start | bytes 32768 | tf_op jit(solution)/shard_map/all_to_all | solution.py:239
  67.3 7.1 %all-to-all-done.figures_ref = f32[32,1,128]{2,1,0:T(1,128)S(1)} async-done(((f32[32,1,128]{2,1,0:T(1,128)}), f32[32,1,128]{2,1,0:T(1,128)S(1)}, u32[]{:S(2)}, u32[]{:S(2)}) %all-to-all-start) | async-done | bytes 16416 | tf_op jit(solution)/shard_map/all_to_all | solution.py:239
  74.4 1.2 copy-done.3
  75.6 2.0 %shard_map.111 = (bf16[64,1024]{1,0:T(8,128)(2,1)S(1)}, bf16[64,1024]{1,0:T(8,128)(2,1)S(1)}, bf16[64,1024]{1,0:T(8,128)(2,1)S(1)}, bf16[64,1024]{1,0:T(8,128)(2...) custom-call(s32[4]{0:T(128)S(1)} %iota_xor_fusion.order_ref, f32[32,1,128]{2,1,0:T(1,128)S(1)} %all-to-all-done.figures_ref, ...), custom_call_target="tpu_custom_call" | custom-call | tf_op jit(solution)/shard_map/pallas_call | solution.py:184
  77.6 0.6 collective-permute-start.6
  78.2 0.5 collective-permute-start.13
  78.7 0.6 collective-permute-start.9
  79.4 0.5 collective-permute-start.7
  79.9 4.1 %collective-permute-done.6.refs_1_ = bf16[64,1024]{1,0:T(8,128)(2,1)S(1)} collective-permute-done((bf16[64,1024]{1,0:T(8,128)(2,1)S(1)}, bf16[64,1024]{1,0:T(8,128)(2,1)S(1)}, u32[]{:S(2)}, u32[]{:S(2)}) %collective-permute-start.6) | collective-permute-done | bytes 131104 | tf_op jit(solution)/shard_map/ppermute | solution.py:195
  83.9 0.5 collective-permute-start.10
  84.4 0.2 collective-permute-start.8
  84.6 0.0 collective-permute-done.13.refs_8_
  84.6 0.0 collective-permute-done.9.refs_4_
  84.6 1.5 %collective-permute-start.11 = (bf16[64,1024]{1,0:T(8,128)(2,1)S(1)}, bf16[64,1024]{1,0:T(8,128)(2,1)S(1)}, u32[]{:S(2)}, u32[]{:S(2)}) collective-permute-start(bf16[64,1024]{1,0:T(8,128)(2,1)S(1)} %collective-permute-done.9.refs_4_), channel_id=1, source_target_pairs={{0,4},{2,6},{4,0},{6,2},{1,5},{3,7},{5,1},{7,3},{8,12},{10,14},{12... | collective-permute-start | bytes 393224 | tf_op jit(solution)/shard_map/ppermute | solution.py:195
  86.1 0.5 collective-permute-start.14
  86.6 4.7 %collective-permute-done.7.refs_2_ = bf16[64,1024]{1,0:T(8,128)(2,1)S(1)} collective-permute-done((bf16[64,1024]{1,0:T(8,128)(2,1)S(1)}, bf16[64,1024]{1,0:T(8,128)(2,1)S(1)}, u32[]{:S(2)}, u32[]{:S(2)}) %collective-permute-start.7) | collective-permute-done | bytes 131104 | tf_op jit(solution)/shard_map/ppermute | solution.py:195
  91.4 1.4 %collective-permute-start.17 = (bf16[64,1024]{1,0:T(8,128)(2,1)S(1)}, bf16[64,1024]{1,0:T(8,128)(2,1)S(1)}, u32[]{:S(2)}, u32[]{:S(2)}) collective-permute-start(bf16[64,1024]{1,0:T(8,128)(2,1)S(1)} %collective-permute-done.7.refs_2_), channel_id=1, source_target_pairs={{0,4},{2,6},{4,0},{6,2},{1,5},{3,7},{5,1},{7,3},{8,12},{10,14},{12... | collective-permute-start | bytes 393224 | tf_op jit(solution)/shard_map/ppermute | solution.py:195
  92.7 0.0 collective-permute-done.11.refs_12_
  92.8 0.6 copy-done.5
  93.4 0.0 collective-permute-done.14.refs_9_
  93.4 1.5 %collective-permute-start.15 = (bf16[64,1024]{1,0:T(8,128)(2,1)S(1)}, bf16[64,1024]{1,0:T(8,128)(2,1)S(1)}, u32[]{:S(2)}, u32[]{:S(2)}) collective-permute-start(bf16[64,1024]{1,0:T(8,128)(2,1)S(1)} %collective-permute-done.14.refs_9_), channel_id=1, source_target_pairs={{0,2},{2,0},{4,6},{6,4},{1,3},{3,1},{5,7},{7,5},{8,10},{10,8},{12,... | collective-permute-start | bytes 393224 | tf_op jit(solution)/shard_map/ppermute | solution.py:195
  94.9 0.7 copy-done.7
  95.5 0.5 collective-permute-start.12
  96.1 1.1 collective-permute-done.17.refs_10_
  97.2 0.7 copy-done.9
  97.9 1.3 collective-permute-start.18
  99.2 0.2 collective-permute-done.15.refs_13_
  99.4 0.6 copy-done.11
  100.1 1.8 %collective-permute-start.16 = (bf16[64,1024]{1,0:T(8,128)(2,1)S(1)}, bf16[64,1024]{1,0:T(8,128)(2,1)}, u32[]{:S(2)}, u32[]{:S(2)}) collective-permute-start(bf16[64,1024]{1,0:T(8,128)(2,1)S(1)} %collective-permute-done.8.refs_3_), channel_id=1, source_target_pairs={{0,2},{2,0},{4,6},{6,4},{1,3},{3,1},{5,7},{7,5},{8,10},{10,8},{12,... | collective-permute-start | bytes 393224 | tf_op jit(solution)/shard_map/ppermute | solution.py:195
  101.9 0.0 collective-permute-start.19
  101.9 1.0 collective-permute-done.18.refs_11_
  102.9 1.4 %collective-permute-start.20 = (bf16[64,1024]{1,0:T(8,128)(2,1)}, bf16[64,1024]{1,0:T(8,128)(2,1)}, u32[]{:S(2)}, u32[]{:S(2)}) collective-permute-start(bf16[64,1024]{1,0:T(8,128)(2,1)} %collective-permute-done.18.refs_11_), channel_id=1, source_target_pairs={{0,2},{2,0},{4,6},{6,4},{1,3},{3,1},{5,7},{7,5},{8,10},{10,8},{12,... | collective-permute-start | bytes 393224 | tf_op jit(solution)/shard_map/ppermute | solution.py:195
  104.3 0.8 collective-permute-done.16.refs_7_
  105.1 2.1 %collective-permute-done.19.refs_14_ = bf16[64,1024]{1,0:T(8,128)(2,1)} collective-permute-done((bf16[64,1024]{1,0:T(8,128)(2,1)}, bf16[64,1024]{1,0:T(8,128)(2,1)}, u32[]{:S(2)}, u32[]{:S(2)}) %collective-permute-start.19) | collective-permute-done | bytes 131104 | tf_op jit(solution)/shard_map/ppermute | solution.py:195
  107.2 1.0 collective-permute-done.20.refs_15_
  108.2 0.9 copy-done.6
  109.1 0.9 copy-done.8
  110.0 0.9 copy-done.10
  110.9 0.9 copy-done.12
  111.8 11.3 %shard_map.112 = (bf16[64,1024]{1,0:T(8,128)(2,1)S(1)}, bf16[64,1024]{1,0:T(8,128)(2,1)S(1)}, bf16[64,1024]{1,0:T(8,128)(2,1)S(1)}, bf16[64,1024]{1,0:T(8,128)(2,1)S(1)}) custom-call(bf16[64,1024]{1,0:T(8,128)(2,1)S(1)} %get-tuple-element.75.refs_0_, bf16[64,1024]{1,0:T(8,128)(2,1)S(1)} %collective-permute-done.6.refs_1_, ...), custom_call_target="tpu_custom_call" | custom-call | tf_op jit(solution)/shard_map/pallas_call | solution.py:85
  123.2 0.5 slice.3
  123.7 0.6 collective-permute-start.21
  124.3 1.5 %collective-permute-start.22 = (bf16[64,1024]{1,0:T(8,128)(2,1)S(1)}, bf16[64,1024]{1,0:T(8,128)(2,1)S(1)}, u32[]{:S(2)}, u32[]{:S(2)}) collective-permute-start(bf16[64,1024]{1,0:T(8,128)(2,1)S(1)} %get-tuple-element.86), channel_id=1, source_target_pairs={{0,16},{8,24},{16,0},{24,8},{1,17},{9,25},{17,1},{25,9},{2,18},{10... | collective-permute-start | bytes 393224 | tf_op jit(solution)/shard_map/ppermute | solution.py:195
  125.8 2.3 %collective-permute-start.23 = (bf16[64,1024]{1,0:T(8,128)(2,1)S(1)}, bf16[64,1024]{1,0:T(8,128)(2,1)S(1)}, u32[]{:S(2)}, u32[]{:S(2)}) collective-permute-start(bf16[64,1024]{1,0:T(8,128)(2,1)S(1)} %get-tuple-element.87), channel_id=1, source_target_pairs={{0,24},{8,16},{16,8},{24,0},{1,25},{9,17},{17,9},{25,1},{2,26},{10... | collective-permute-start | bytes 393224 | tf_op jit(solution)/shard_map/ppermute | solution.py:195
  128.1 2.0 %multiply_subtract_fusion = (f32[1,4,64]{2,1,0:T(4,128)}, f32[1,4,64]{2,1,0:T(4,128)}) fusion(f32[1,4,64]{2,1,0:T(4,128)S(1)} %copy-done.14, f32[1,4,64]{2,1,0:T(4,128)} %param.13, f32[4,256]{1,0:T(4,128)S(1)} %get-tuple-element.92, s32[]{:T(128)S(6)} %select_n.20, f32[]{:T(128)} %bitcast.13, f32[1,4,64]{2,1,0:T(4,128)} %param.12), kind=kLoop, calls=%fused_computation.11 | loop fusion | flops 3328 | bytes 6152 | tf_op jit(solution)/shard_map/sub | solution.py:294
  130.1 2.9 %collective-permute-done.22.refs_2_ = bf16[64,1024]{1,0:T(8,128)(2,1)S(1)} collective-permute-done((bf16[64,1024]{1,0:T(8,128)(2,1)S(1)}, bf16[64,1024]{1,0:T(8,128)(2,1)S(1)}, u32[]{:S(2)}, u32[]{:S(2)}) %collective-permute-start.22) | collective-permute-done | bytes 131104 | tf_op jit(solution)/shard_map/ppermute | solution.py:195
  133.0 1.6 %shard_map.113 = (bf16[4,64,1024]{2,1,0:T(8,128)(2,1)}, bf16[4,64,1024]{2,1,0:T(8,128)(2,1)}) custom-call(s32[4]{0:T(128)S(1)} %iota_xor_fusion.order_ref, bf16[64,1024]{1,0:T(8,128)(2,1)S(1)} %get-tuple-element.84.refs_0_, bf16[64,1024]{1,0:T(8,128)(2,1)S(1)} %collective-permute-done.21.refs_1_, bf16[64,1024]{1,0:T(8,128)(2,1)S(1)} %collective-permute-done.22.refs_2_, ...), custom_call_target="tpu_custom_call" | custom-call | tf_op jit(solution)/shard_map/pallas_call | solution.py:184
  (27 shorter events, 0.1 us)
Async XLA Ops:
  0.6 5.8 %copy-start = (bf16[1,1,4,256,1024]{4,3,2,1,0:T(8,128)(2,1)S(1)}, bf16[1,1,4,256,1024]{4,3,2,1,0:T(8,128)(2,1)}, u32[]{:S(2)}) copy-start(bf16[1,1,4,256,1024]{4,3,2,1,0:T(8,128)(2,1)} %param.7) | copy-start | bytes 6291460
  0.6 6.9 %collective-permute-start.2 = (bf16[4,256]{1,0:T(4,128)(2,1)}, bf16[4,256]{1,0:T(4,128)(2,1)S(1)}, u32[]{:S(2)}, u32[]{:S(2)}) collective-permute-start(bf16[4,256]{1,0:T(4,128)(2,1)} %bitcast.49), channel_id=1, source_target_pairs={{0,24},{8,16},{16,8},{24,0},{1,25},{9,17},{17,9},{25,1},{2,26},{10... | collective-permute-start | bytes 6152 | tf_op jit(solution)/shard_map/ppermute | solution.py:195
  5.8 4.7 %collective-permute-start.1 = (bf16[4,256]{1,0:T(4,128)(2,1)}, bf16[4,256]{1,0:T(4,128)(2,1)S(1)}, u32[]{:S(2)}, u32[]{:S(2)}) collective-permute-start(bf16[4,256]{1,0:T(4,128)(2,1)} %bitcast.50), channel_id=1, source_target_pairs={{0,16},{8,24},{16,0},{24,8},{1,17},{9,25},{17,1},{25,9},{2,18},{10... | collective-permute-start | bytes 6152 | tf_op jit(solution)/shard_map/ppermute | solution.py:195
  5.8 4.7 %collective-permute-start = (bf16[4,256]{1,0:T(4,128)(2,1)}, bf16[4,256]{1,0:T(4,128)(2,1)S(1)}, u32[]{:S(2)}, u32[]{:S(2)}) collective-permute-start(bf16[4,256]{1,0:T(4,128)(2,1)} %bitcast.51), channel_id=1, source_target_pairs={{0,8},{8,0},{16,24},{24,16},{1,9},{9,1},{17,25},{25,17},{2,10},{10... | collective-permute-start | bytes 6152 | tf_op jit(solution)/shard_map/ppermute | solution.py:195
  6.4 44.3 %copy-start.1 = (f32[1,4,64,1024]{3,2,1,0:T(8,128)S(1)}, f32[1,4,64,1024]{3,2,1,0:T(8,128)}, u32[]{:S(2)}) copy-start(f32[1,4,64,1024]{3,2,1,0:T(8,128)} %param.9) | copy-start | bytes 3145732
  6.4 44.3 %copy-start.13 = (bf16[1,1,4,256]{3,2,1,0:T(4,128)(2,1)S(1)}, bf16[1,1,4,256]{3,2,1,0:T(4,128)(2,1)}, u32[]{:S(2)}) copy-start(bf16[1,1,4,256]{3,2,1,0:T(4,128)(2,1)} %param.8) | copy-start | bytes 6148
  12.1 23.2 %collective-permute-start.3 = (bf16[4,64,1024]{2,1,0:T(8,128)(2,1)}, bf16[4,64,1024]{2,1,0:T(8,128)(2,1)}, u32[]{:S(2)}, u32[]{:S(2)}) collective-permute-start(bf16[4,64,1024]{2,1,0:T(8,128)(2,1)} %dynamic-slice_bitcast_fusion.1), channel_id=1, source_target_pairs={{0,8},{8,0},{16,24},{24,16},{1,9},{9,1},{17,25},{25,17},{2,10},{10... | collective-permute-start | bytes 1572872 | tf_op jit(solution)/shard_map/ppermute | solution.py:195
  12.1 38.5 %collective-permute-start.4 = (bf16[4,64,1024]{2,1,0:T(8,128)(2,1)}, bf16[4,64,1024]{2,1,0:T(8,128)(2,1)}, u32[]{:S(2)}, u32[]{:S(2)}) collective-permute-start(bf16[4,64,1024]{2,1,0:T(8,128)(2,1)} %dynamic-slice_bitcast_fusion.2), channel_id=1, source_target_pairs={{0,16},{8,24},{16,0},{24,8},{1,17},{9,25},{17,1},{25,9},{2,18},{10... | collective-permute-start | bytes 1572872 | tf_op jit(solution)/shard_map/ppermute | solution.py:195
  14.2 36.5 %collective-permute-start.5 = (bf16[4,64,1024]{2,1,0:T(8,128)(2,1)}, bf16[4,64,1024]{2,1,0:T(8,128)(2,1)}, u32[]{:S(2)}, u32[]{:S(2)}) collective-permute-start(bf16[4,64,1024]{2,1,0:T(8,128)(2,1)} %dynamic-slice_bitcast_fusion.3), channel_id=1, source_target_pairs={{0,24},{8,16},{16,8},{24,0},{1,25},{9,17},{17,9},{25,1},{2,26},{10... | collective-permute-start | bytes 1572872 | tf_op jit(solution)/shard_map/ppermute | solution.py:195
  53.4 1.0 copy-start.2
  54.4 20.0 %all-to-all-start = ((f32[32,1,128]{2,1,0:T(1,128)}), f32[32,1,128]{2,1,0:T(1,128)S(1)}, u32[]{:S(2)}, u32[]{:S(2)}) async-start(f32[32,1,128]{2,1,0:T(1,128)} %bitcast.8), calls=%async_computation | async-start | bytes 32768 | tf_op jit(solution)/shard_map/all_to_all | solution.py:239
  74.4 1.2 copy-start.3
  75.6 52.5 %copy-start.14 = (f32[1,4,64]{2,1,0:T(4,128)S(1)}, f32[1,4,64]{2,1,0:T(4,128)}, u32[]{:S(2)}) copy-start(f32[1,4,64]{2,1,0:T(4,128)} %param.11) | copy-start | bytes 3076
  77.6 55.4 %copy-start.4 = (bf16[1,4,64,1024]{3,2,1,0:T(8,128)(2,1)S(1)}, bf16[1,4,64,1024]{3,2,1,0:T(8,128)(2,1)}, u32[]{:S(2)}) copy-start(bf16[1,4,64,1024]{3,2,1,0:T(8,128)(2,1)} %param.10) | copy-start | bytes 1572868
  77.6 6.3 %collective-permute-start.6 = (bf16[64,1024]{1,0:T(8,128)(2,1)S(1)}, bf16[64,1024]{1,0:T(8,128)(2,1)S(1)}, u32[]{:S(2)}, u32[]{:S(2)}) collective-permute-start(bf16[64,1024]{1,0:T(8,128)(2,1)S(1)} %get-tuple-element.76), channel_id=1, source_target_pairs={{0,8},{8,0},{16,24},{24,16},{1,9},{9,1},{17,25},{25,17},{2,10},{10... | collective-permute-start | bytes 393224 | tf_op jit(solution)/shard_map/ppermute | solution.py:195
  78.2 6.4 %collective-permute-start.13 = (bf16[64,1024]{1,0:T(8,128)(2,1)S(1)}, bf16[64,1024]{1,0:T(8,128)(2,1)S(1)}, u32[]{:S(2)}, u32[]{:S(2)}) collective-permute-start(bf16[64,1024]{1,0:T(8,128)(2,1)S(1)} %get-tuple-element.75.refs_0_), channel_id=1, source_target_pairs={{0,4},{2,6},{4,0},{6,2},{1,5},{3,7},{5,1},{7,3},{8,12},{10,14},{12... | collective-permute-start | bytes 393224 | tf_op jit(solution)/shard_map/ppermute | solution.py:195
  78.7 5.8 %collective-permute-start.9 = (bf16[64,1024]{1,0:T(8,128)(2,1)S(1)}, bf16[64,1024]{1,0:T(8,128)(2,1)S(1)}, u32[]{:S(2)}, u32[]{:S(2)}) collective-permute-start(bf16[64,1024]{1,0:T(8,128)(2,1)S(1)} %get-tuple-element.75.refs_0_), channel_id=1, source_target_pairs={{0,2},{2,0},{4,6},{6,4},{1,3},{3,1},{5,7},{7,5},{8,10},{10,8},{12,... | collective-permute-start | bytes 393224 | tf_op jit(solution)/shard_map/ppermute | solution.py:195
  79.4 12.0 %collective-permute-start.7 = (bf16[64,1024]{1,0:T(8,128)(2,1)S(1)}, bf16[64,1024]{1,0:T(8,128)(2,1)S(1)}, u32[]{:S(2)}, u32[]{:S(2)}) collective-permute-start(bf16[64,1024]{1,0:T(8,128)(2,1)S(1)} %get-tuple-element.77), channel_id=1, source_target_pairs={{0,16},{8,24},{16,0},{24,8},{1,17},{9,25},{17,1},{25,9},{2,18},{10... | collective-permute-start | bytes 393224 | tf_op jit(solution)/shard_map/ppermute | solution.py:195
  83.9 7.4 %collective-permute-start.10 = (bf16[64,1024]{1,0:T(8,128)(2,1)S(1)}, bf16[64,1024]{1,0:T(8,128)(2,1)S(1)}, u32[]{:S(2)}, u32[]{:S(2)}) collective-permute-start(bf16[64,1024]{1,0:T(8,128)(2,1)S(1)} %collective-permute-done.6.refs_1_), channel_id=1, source_target_pairs={{0,2},{2,0},{4,6},{6,4},{1,3},{3,1},{5,7},{7,5},{8,10},{10,8},{12,... | collective-permute-start | bytes 393224 | tf_op jit(solution)/shard_map/ppermute | solution.py:195
  84.4 11.7 %collective-permute-start.8 = (bf16[64,1024]{1,0:T(8,128)(2,1)S(1)}, bf16[64,1024]{1,0:T(8,128)(2,1)S(1)}, u32[]{:S(2)}, u32[]{:S(2)}) collective-permute-start(bf16[64,1024]{1,0:T(8,128)(2,1)S(1)} %get-tuple-element.78), channel_id=1, source_target_pairs={{0,24},{8,16},{16,8},{24,0},{1,25},{9,17},{17,9},{25,1},{2,26},{10... | collective-permute-start | bytes 393224 | tf_op jit(solution)/shard_map/ppermute | solution.py:195
  84.6 8.2 %collective-permute-start.11 = (bf16[64,1024]{1,0:T(8,128)(2,1)S(1)}, bf16[64,1024]{1,0:T(8,128)(2,1)S(1)}, u32[]{:S(2)}, u32[]{:S(2)}) collective-permute-start(bf16[64,1024]{1,0:T(8,128)(2,1)S(1)} %collective-permute-done.9.refs_4_), channel_id=1, source_target_pairs={{0,4},{2,6},{4,0},{6,2},{1,5},{3,7},{5,1},{7,3},{8,12},{10,14},{12... | collective-permute-start | bytes 393224 | tf_op jit(solution)/shard_map/ppermute | solution.py:195
  86.1 7.3 %collective-permute-start.14 = (bf16[64,1024]{1,0:T(8,128)(2,1)S(1)}, bf16[64,1024]{1,0:T(8,128)(2,1)S(1)}, u32[]{:S(2)}, u32[]{:S(2)}) collective-permute-start(bf16[64,1024]{1,0:T(8,128)(2,1)S(1)} %collective-permute-done.6.refs_1_), channel_id=1, source_target_pairs={{0,4},{2,6},{4,0},{6,2},{1,5},{3,7},{5,1},{7,3},{8,12},{10,14},{12... | collective-permute-start | bytes 393224 | tf_op jit(solution)/shard_map/ppermute | solution.py:195
  91.4 5.9 %collective-permute-start.17 = (bf16[64,1024]{1,0:T(8,128)(2,1)S(1)}, bf16[64,1024]{1,0:T(8,128)(2,1)S(1)}, u32[]{:S(2)}, u32[]{:S(2)}) collective-permute-start(bf16[64,1024]{1,0:T(8,128)(2,1)S(1)} %collective-permute-done.7.refs_2_), channel_id=1, source_target_pairs={{0,4},{2,6},{4,0},{6,2},{1,5},{3,7},{5,1},{7,3},{8,12},{10,14},{12... | collective-permute-start | bytes 393224 | tf_op jit(solution)/shard_map/ppermute | solution.py:195
  92.7 0.6 copy-start.5
  93.4 6.0 %collective-permute-start.15 = (bf16[64,1024]{1,0:T(8,128)(2,1)S(1)}, bf16[64,1024]{1,0:T(8,128)(2,1)S(1)}, u32[]{:S(2)}, u32[]{:S(2)}) collective-permute-start(bf16[64,1024]{1,0:T(8,128)(2,1)S(1)} %collective-permute-done.14.refs_9_), channel_id=1, source_target_pairs={{0,2},{2,0},{4,6},{6,4},{1,3},{3,1},{5,7},{7,5},{8,10},{10,8},{12,... | collective-permute-start | bytes 393224 | tf_op jit(solution)/shard_map/ppermute | solution.py:195
  94.9 0.7 copy-start.7
  95.5 6.4 %collective-permute-start.12 = (bf16[64,1024]{1,0:T(8,128)(2,1)S(1)}, bf16[64,1024]{1,0:T(8,128)(2,1)}, u32[]{:S(2)}, u32[]{:S(2)}) collective-permute-start(bf16[64,1024]{1,0:T(8,128)(2,1)S(1)} %collective-permute-done.7.refs_2_), channel_id=1, source_target_pairs={{0,2},{2,0},{4,6},{6,4},{1,3},{3,1},{5,7},{7,5},{8,10},{10,8},{12,... | collective-permute-start | bytes 393224 | tf_op jit(solution)/shard_map/ppermute | solution.py:195
  97.2 0.7 copy-start.9
  97.9 5.1 %collective-permute-start.18 = (bf16[64,1024]{1,0:T(8,128)(2,1)S(1)}, bf16[64,1024]{1,0:T(8,128)(2,1)}, u32[]{:S(2)}, u32[]{:S(2)}) collective-permute-start(bf16[64,1024]{1,0:T(8,128)(2,1)S(1)} %collective-permute-done.8.refs_3_), channel_id=1, source_target_pairs={{0,4},{2,6},{4,0},{6,2},{1,5},{3,7},{5,1},{7,3},{8,12},{10,14},{12... | collective-permute-start | bytes 393224 | tf_op jit(solution)/shard_map/ppermute | solution.py:195
  99.4 0.6 copy-start.11
  100.1 5.1 %collective-permute-start.16 = (bf16[64,1024]{1,0:T(8,128)(2,1)S(1)}, bf16[64,1024]{1,0:T(8,128)(2,1)}, u32[]{:S(2)}, u32[]{:S(2)}) collective-permute-start(bf16[64,1024]{1,0:T(8,128)(2,1)S(1)} %collective-permute-done.8.refs_3_), channel_id=1, source_target_pairs={{0,2},{2,0},{4,6},{6,4},{1,3},{3,1},{5,7},{7,5},{8,10},{10,8},{12,... | collective-permute-start | bytes 393224 | tf_op jit(solution)/shard_map/ppermute | solution.py:195
  101.9 5.3 %collective-permute-start.19 = (bf16[64,1024]{1,0:T(8,128)(2,1)}, bf16[64,1024]{1,0:T(8,128)(2,1)}, u32[]{:S(2)}, u32[]{:S(2)}) collective-permute-start(bf16[64,1024]{1,0:T(8,128)(2,1)} %collective-permute-done.12.refs_6_), channel_id=1, source_target_pairs={{0,4},{2,6},{4,0},{6,2},{1,5},{3,7},{5,1},{7,3},{8,12},{10,14},{12... | collective-permute-start | bytes 393224 | tf_op jit(solution)/shard_map/ppermute | solution.py:195
  102.9 5.3 %collective-permute-start.20 = (bf16[64,1024]{1,0:T(8,128)(2,1)}, bf16[64,1024]{1,0:T(8,128)(2,1)}, u32[]{:S(2)}, u32[]{:S(2)}) collective-permute-start(bf16[64,1024]{1,0:T(8,128)(2,1)} %collective-permute-done.18.refs_11_), channel_id=1, source_target_pairs={{0,2},{2,0},{4,6},{6,4},{1,3},{3,1},{5,7},{7,5},{8,10},{10,8},{12,... | collective-permute-start | bytes 393224 | tf_op jit(solution)/shard_map/ppermute | solution.py:195
  108.2 0.9 copy-start.6
  109.1 0.9 copy-start.8
  110.0 0.9 copy-start.10
  110.9 0.9 copy-start.12
  123.7 6.4 %collective-permute-start.21 = (bf16[64,1024]{1,0:T(8,128)(2,1)S(1)}, bf16[64,1024]{1,0:T(8,128)(2,1)S(1)}, u32[]{:S(2)}, u32[]{:S(2)}) collective-permute-start(bf16[64,1024]{1,0:T(8,128)(2,1)S(1)} %get-tuple-element.85), channel_id=1, source_target_pairs={{0,8},{8,0},{16,24},{24,16},{1,9},{9,1},{17,25},{25,17},{2,10},{10... | collective-permute-start | bytes 393224 | tf_op jit(solution)/shard_map/ppermute | solution.py:195
  124.3 8.7 %collective-permute-start.22 = (bf16[64,1024]{1,0:T(8,128)(2,1)S(1)}, bf16[64,1024]{1,0:T(8,128)(2,1)S(1)}, u32[]{:S(2)}, u32[]{:S(2)}) collective-permute-start(bf16[64,1024]{1,0:T(8,128)(2,1)S(1)} %get-tuple-element.86), channel_id=1, source_target_pairs={{0,16},{8,24},{16,0},{24,8},{1,17},{9,25},{17,1},{25,9},{2,18},{10... | collective-permute-start | bytes 393224 | tf_op jit(solution)/shard_map/ppermute | solution.py:195
  125.8 7.2 %collective-permute-start.23 = (bf16[64,1024]{1,0:T(8,128)(2,1)S(1)}, bf16[64,1024]{1,0:T(8,128)(2,1)S(1)}, u32[]{:S(2)}, u32[]{:S(2)}) collective-permute-start(bf16[64,1024]{1,0:T(8,128)(2,1)S(1)} %get-tuple-element.87), channel_id=1, source_target_pairs={{0,24},{8,16},{16,8},{24,0},{1,25},{9,17},{17,9},{25,1},{2,26},{10... | collective-permute-start | bytes 393224 | tf_op jit(solution)/shard_map/ppermute | solution.py:195

commit v2 on v1

--- a/solution.py
+++ b/solution.py
@@ -90,7 +90,7 @@
             pltpu.VMEM((count, pieces * height, width), jnp.bfloat16),
             pltpu.VMEM((count, pieces * height, width), jnp.bfloat16),
         ],
-        compiler_params=pltpu.CompilerParams(vmem_limit_bytes=24 * MIB),
+        compiler_params=pltpu.CompilerParams(vmem_limit_bytes=32 * MIB),
     )(*[piece for block in blocks for piece in block])
 
 
@@ -102,13 +102,39 @@
     return total
 
 
-def sum_kernel(shard_count, section_ref, *refs):
+def slices_kernel(count, place_ref, grad_ref, *refs):
+    outputs, semaphores = refs[:count], refs[count]
+    copies = [
+        pltpu.make_async_copy(
+            grad_ref.at[:, place_ref[offset]], outputs[offset], semaphores.at[offset]
+        )
+        for offset in range(count)
+    ]
+    for copy in reversed(copies):
+        copy.start()
+    for copy in reversed(copies):
+        copy.wait()
+
+
+def row_slices(place, by_rows):
+    matrix_count, shard_count, height, width = by_rows.shape
+    return pl.pallas_call(
+        functools.partial(slices_kernel, shard_count),
+        out_shape=[jax.ShapeDtypeStruct((matrix_count, height, width), by_rows.dtype)]
+        * shard_count,
+        in_specs=[
+            pl.BlockSpec(memory_space=pltpu.SMEM),
+            pl.BlockSpec(memory_space=pltpu.HBM),
+        ],
+        out_specs=[pl.BlockSpec(memory_space=pltpu.HBM)] * shard_count,
+        scratch_shapes=[pltpu.SemaphoreType.DMA((shard_count,))],
+    )(place, by_rows)
+
+
+def sum_kernel(shard_count, place_ref, *refs):
     parts = refs[:shard_count]
-    vector_parts = refs[shard_count : 2 * shard_count]
-    momentum_ref, grad_ref, vector_ref, figures_ref = refs[2 * shard_count :]
-    vector = vector_parts[0][...].astype(jnp.float32)
-    for part in vector_parts[1:]:
-        vector = vector + part[...].astype(jnp.float32)
+    vector_parts, momentum_ref, grad_ref, vector_ref, figures_ref = refs[shard_count:]
+    vector = jnp.sum(vector_parts[...].astype(jnp.float32), axis=0)
     vector_ref[...] = vector
     total = folded(vector * vector) * (1.0 / shard_count)
     squares, crosses, momentum_squares = [], [], []
@@ -131,13 +157,13 @@
     line = jnp.sum(jnp.where(line_index == lane_index, sums, 0.0), axis=0, keepdims=True)
     total_only = jnp.where(lane_index[:1] == 3 * momentum_ref.shape[0], line, 0.0)
     for section in range(figures_ref.shape[1]):
-        chosen = jnp.where(section_ref[0] == section, line, total_only)
+        chosen = jnp.where(place_ref[shard_count] == section, line, total_only)
         figures_ref[:, section] = jnp.broadcast_to(
             chosen[None], (figures_ref.shape[0],) + line.shape
         )
 
 
-def scale_kernel(matrix_count, order_ref, figures_ref, grad_ref, momentum_ref, *refs):
+def scale_kernel(matrix_count, place_ref, figures_ref, grad_ref, momentum_ref, *refs):
     outputs = refs[:matrix_count]
     clip_ref, new_momentum_ref = refs[matrix_count:]
     line = jnp.sum(figures_ref[...], axis=0)
@@ -157,7 +183,7 @@
     inverse = 1.0 / (jnp.sqrt(jnp.maximum(update_norm, 0.0)) + 1e-07)
     position = lax.broadcasted_iota(jnp.int32, inverse.shape, 0)
     for place in range(matrix_count):
-        matrix = order_ref[place]
+        matrix = place_ref[place]
         factor = jnp.sum(jnp.where(position == matrix, inverse, 0.0), axis=0, keepdims=True)
         clipped = clip * grad_ref[matrix]
         new_momentum = mom_beta * momentum_ref[matrix] + clipped
@@ -166,12 +192,12 @@
         outputs[place][...] = (nesterov * factor).astype(jnp.bfloat16)
 
 
-def end_kernel(matrix_count, order_ref, *refs):
+def end_kernel(matrix_count, place_ref, *refs):
     arrived = refs[:matrix_count]
     weights_ref, update_ref, new_weights_ref = refs[matrix_count:]
     step_size = muon_rate * (0.2 * math.sqrt(D))
     for place in range(matrix_count):
-        matrix = order_ref[place]
+        matrix = place_ref[place]
         update = arrived[place][...]
         update_ref[matrix] = update
         new_weights_ref[matrix] = (
@@ -180,13 +206,30 @@
         ).astype(jnp.bfloat16)
 
 
+def vectors_kernel(
+    place_ref, clip_ref, sums_ref, vectors_ref, first_ref, second_ref, direction_ref, new_ref
+):
+    width = vectors_ref.shape[1]
+    count = sums_ref.shape[1] // width
+    rows = sums_ref[:, :width]
+    for position in range(1, count):
+        part = sums_ref[:, position * width : (position + 1) * width]
+        rows = jnp.where(place_ref[0] == position, part, rows)
+    clipped = clip_ref[0:1, 0:1] * rows
+    updated_first = 0.9 * first_ref[...] + 0.1 * clipped
+    updated_second = 0.999 * second_ref[...] + 0.001 * clipped * clipped
+    direction = updated_first / (jnp.sqrt(updated_second) + 1e-08)
+    direction_ref[...] = direction
+    new_ref[...] = vectors_ref[...] * (1.0 - adam_rate * adam_decay) - adam_rate * direction
+
+
 def on_device(kernel, scalars, operands, out_shape):
     return pl.pallas_call(
         kernel,
         out_shape=out_shape,
         in_specs=[pl.BlockSpec(memory_space=pltpu.SMEM)]
         + [pl.BlockSpec(memory_space=pltpu.VMEM)] * len(operands),
-        compiler_params=pltpu.CompilerParams(vmem_limit_bytes=12 * MIB),
+        compiler_params=pltpu.CompilerParams(vmem_limit_bytes=16 * MIB),
     )(scalars, *operands)
 
 
@@ -208,31 +251,35 @@
         return general_device(
             grad_parts, vector_grads, momentum, weights, vectors, first_moment, second_moment
         )
-    shard_index = lax.axis_index("shard")
-    order = shard_index ^ jnp.arange(shard_count, dtype=jnp.int32)
+    vector_count, vector_width = vectors.shape[1:]
     own_momentum = momentum[0]
-    vector_count, vector_width = vectors.shape[1:]
+    position = jnp.arange(shard_count + 1, dtype=jnp.int32)
+    place = jnp.where(
+        position == shard_count,
+        lax.axis_index("section").astype(jnp.int32),
+        lax.axis_index("shard").astype(jnp.int32) ^ position,
+    )
 
     by_rows = grad_parts.reshape(matrix_count, shard_count, local_height, width)
-    own_vectors = vector_grads.reshape(vector_count, shard_count * vector_width)
-    vector_parts = [own_vectors] + [
-        swapped(own_vectors, "shard", offset) for offset in range(1, shard_count)
-    ]
-    parts = [None] * shard_count
-    index = shard_index
-    for offset in reversed(range(shard_count)):
-        rows = lax.dynamic_index_in_dim(by_rows, index ^ offset, 1, keepdims=False)
-        index, rows, vector_parts = lax.optimization_barrier((index, rows, vector_parts))
-        parts[offset] = swapped(rows, "shard", offset) if offset else rows
+    parts = list(row_slices(place, by_rows))
+    for offset in reversed(range(1, shard_count)):
+        parts[offset] = swapped(parts[offset], "shard", offset)
+    vector_parts = lax.all_to_all(
+        jnp.broadcast_to(vector_grads[0], (shard_count, vector_count, vector_width * shard_count)),
+        "shard",
+        split_axis=0,
+        concat_axis=0,
+        tiled=True,
+    )
 
     others = shard_count * tensor_count
     grad_rows, vector_whole, figures = on_device(
         functools.partial(sum_kernel, shard_count),
-        lax.axis_index("section").astype(jnp.int32).reshape(1),
-        parts + vector_parts + [own_momentum],
+        place,
+        parts + [vector_parts, own_momentum],
         [
             jax.ShapeDtypeStruct(own_momentum.shape, jnp.float32),
-            jax.ShapeDtypeStruct(own_vectors.shape, jnp.float32),
+            jax.ShapeDtypeStruct(vector_parts.shape[1:], jnp.float32),
             jax.ShapeDtypeStruct((others, section_count, 1, LANES), jnp.float32),
         ],
     )
@@ -245,7 +292,7 @@
     )
     *scaled, clip_tile, new_momentum = on_device(
         functools.partial(scale_kernel, matrix_count),
-        order,
+        place,
         [figures, grad_rows, own_momentum],
         [jax.ShapeDtypeStruct((local_height, width), jnp.bfloat16)] * matrix_count
         + [
@@ -278,26 +325,23 @@
     ]
     orthogonal_update, new_weights = on_device(
         functools.partial(end_kernel, matrix_count),
-        order,
+        place,
         arrived + [weights[0]],
         [jax.ShapeDtypeStruct(own_momentum.shape, jnp.bfloat16)] * 2,
     )
 
-    clip_factor = after(clip_tile, results[0])[0, 0]
-    vector_rows = lax.dynamic_slice_in_dim(
-        vector_whole, shard_index * vector_width, vector_width, 1
-    )
-    vector_clipped = clip_factor * vector_rows
-    updated_first = 0.9 * first_moment + 0.1 * vector_clipped
-    updated_second = 0.999 * second_moment + 0.001 * vector_clipped * vector_clipped
-    adam_direction = updated_first / (jnp.sqrt(updated_second) + 1e-08)
-    new_vectors = vectors * (1.0 - adam_rate * adam_decay) - adam_rate * adam_direction
+    adam_direction, new_vectors = on_device(
+        vectors_kernel,
+        place,
+        [clip_tile, vector_whole, vectors[0], first_moment[0], second_moment[0]],
+        [jax.ShapeDtypeStruct(vectors.shape[1:], jnp.float32)] * 2,
+    )
     return (
         new_momentum[None],
         orthogonal_update[None],
         new_weights[None],
-        adam_direction,
-        new_vectors,
+        adam_direction[None],
+        new_vectors[None],
     )
 
 

time: 135 us -> 186 us (1.38)
  Pallas kernels: 17.7 us -> 82 us
  blocking collectives: 0 us -> 57.5 us
  waiting for transfers between devices: 62.4 us -> 21.4 us
  starting transfers between devices: 40.3 us -> 22.4 us
  local copies, waits for them, and re-layouts: 11.5 us -> 1.07 us
    pallas_call x0 -> x1, Pallas kernels: none -> 65.5 us  [row_slices(): pl.pallas_call(functools.partial(slices_kernel, shard_count), out_shape=[...]
    all_to_all x0 -> x2, blocking collectives: none -> 57.5 us  [the longest x1 45.8 us: per_device(): lax.all_to_all(jnp.broadcast_to(vector_grads[0], (shard_count, vector_cou...]
    ppermute x24 -> x21, waiting for transfers between devices: 55.4 us -> 21.4 us  [swapped(): return lax.ppermute(array, axis, pairs)]
    all_to_all x1 -> x0, starting transfers between devices: 12.9 us -> none  [per_device(): lax.all_to_all(figures.reshape(others * section_count, 1, LANES), MESH_AX...]
    unnamed x30 -> x16, local copies, waits for them, and re-layouts: 8.42 us -> 1.06 us
    all_to_all x1 -> x0, waiting for transfers between devices: 7.06 us -> none  [per_device(): lax.all_to_all(figures.reshape(others * section_count, 1, LANES), MESH_AX...]
    ppermute x24 -> x21, starting transfers between devices: 27.4 us -> 22.4 us  [swapped(): return lax.ppermute(array, axis, pairs)]
    squeeze x4 -> x0, local copies, waits for them, and re-layouts: 2.52 us -> none  [per_device(): rows = lax.dynamic_index_in_dim(by_rows, index ^ offset, 1, keepdims=False)]
  transfers between devices with their start and end apart: 25 -> 21, of which waited for: 14 -> 9; matrix products, arithmetic and copies ran while one was open for 2% -> 0% of each run, Pallas kernels for 0% -> 1%
where the time goes in v2:
time: 186 us
  Pallas kernels  82 us (44%)
  blocking collectives  57.5 us (31%)
  starting transfers between devices  22.4 us (12%)
  waiting for transfers between devices  21.4 us (12%)
    pallas_call x1, Pallas kernels, row_slices(): pl.pallas_call(functools.partial(slices_kernel, shard_count), out_shape=[...  65.5 us
    all_to_all x1, blocking collectives, per_device(): lax.all_to_all(jnp.broadcast_to(vector_grads[0], (shard_count, vector_cou...  45.8 us
    ppermute x21, starting transfers between devices, swapped(): return lax.ppermute(array, axis, pairs)  22.4 us
    ppermute x21, waiting for transfers between devices, swapped(): return lax.ppermute(array, axis, pairs)  21.4 us
    all_to_all x1, blocking collectives, per_device(): lax.all_to_all(figures.reshape(others * section_count, 1, LANES), MESH_AX...  11.7 us
    pallas_call x1, Pallas kernels, orthogonalize(): pl.pallas_call(functools.partial(orthogonalize_kernel, count, pieces), ou...  10.2 us
    pallas_call x4, Pallas kernels, on_device(): pl.pallas_call(kernel, out_shape=out_shape, in_specs=[pl.BlockSpec(memory...  6.39 us
  transfers between devices with their start and end apart: 21, of which 9 were waited for; matrix products, arithmetic and copies ran while one was open for 0% of the time, Pallas kernels for 1%

profile of v2, /device:TPU:0, one launch (start us, length us, event | category | flops | bytes accessed | tf_op | source)
XLA Modules:
  0.0 185.6 jit_solution(11233943182662720984)
XLA Ops:
  0.6 0.0 copy-start.7
  0.6 0.0 copy-start
  0.7 0.5 compare_select_fusion.place_ref
  1.2 0.0 copy-start.3
  1.2 65.5 %shard_map.110 = (bf16[4,64,1024]{2,1,0:T(8,128)(2,1)}, bf16[4,64,1024]{2,1,0:T(8,128)(2,1)}, bf16[4,64,1024]{2,1,0:T(8,128)(2,1)}, bf16[4,64,1024]{2,1,0:T(8,128)(2,1)}) custom-call(s32[5]{0:T(128)} %compare_select_fusion.place_ref, bf16[4,4,64,1024]{3,2,1,0:T(8,128)(2,1)} %bitcast.20), custom_call_target="tpu_custom_call" | custom-call | tf_op jit(solution)/shard_map/pallas_call | solution.py:121
  66.6 3.1 %collective-permute-start = (bf16[4,64,1024]{2,1,0:T(8,128)(2,1)}, bf16[4,64,1024]{2,1,0:T(8,128)(2,1)S(1)}, u32[]{:S(2)}, u32[]{:S(2)}) collective-permute-start(bf16[4,64,1024]{2,1,0:T(8,128)(2,1)} %get-tuple-element.32), channel_id=1, source_target_pairs={{0,8},{8,0},{16,24},{24,16},{1,9},{9,1},{17,25},{25,17},{2,10},{10... | collective-permute-start | bytes 1572872 | tf_op jit(solution)/shard_map/ppermute | solution.py:238
  69.7 2.6 %collective-permute-start.1 = (bf16[4,64,1024]{2,1,0:T(8,128)(2,1)}, bf16[4,64,1024]{2,1,0:T(8,128)(2,1)S(1)}, u32[]{:S(2)}, u32[]{:S(2)}) collective-permute-start(bf16[4,64,1024]{2,1,0:T(8,128)(2,1)} %get-tuple-element.33), channel_id=1, source_target_pairs={{0,16},{8,24},{16,0},{24,8},{1,17},{9,25},{17,1},{25,9},{2,18},{10... | collective-permute-start | bytes 1572872 | tf_op jit(solution)/shard_map/ppermute | solution.py:238
  72.3 0.0 collective-permute-start.2
  72.3 0.0 copy-done.7
  72.3 45.8 %all_to_all.10.refs_4_ = bf16[4,4,256]{2,1,0:T(4,128)(2,1)S(1)} all-to-all(bf16[4,4,256]{2,1,0:T(4,128)(2,1)S(1)} %broadcast_in_dim.28), channel_id=1, replica_groups=mesh['shard'=4,'tensor'=4,'section'=2] {'shard'}, dimensions={0} | all-to-all | bytes 16384 | tf_op jit(solution)/shard_map/all_to_all | solution.py:267
  118.2 0.0 collective-permute-done.refs_1_
  118.2 0.0 collective-permute-done.1.refs_2_
  118.2 0.0 collective-permute-done.2.refs_3_
  118.2 0.0 copy-done
  118.2 0.0 copy-done.3
  118.2 0.0 copy-start.2
  118.2 1.0 copy-done.2
  119.2 1.3 shard_map.111
  120.6 11.7 %all_to_all.11.figures_ref = f32[32,1,128]{2,1,0:T(1,128)S(1)} all-to-all(f32[32,1,128]{2,1,0:T(1,128)S(1)} %bitcast.16), channel_id=1, replica_groups=mesh['shard'=4,'tensor'=4,'section'=2] {'shard','tensor','section'}, dimensions={0} | all-to-all | bytes 32768 | tf_op jit(solution)/shard_map/all_to_all | solution.py:286
  132.3 0.0 copy-start.4
  132.3 2.0 %shard_map.112 = (bf16[64,1024]{1,0:T(8,128)(2,1)S(1)}, bf16[64,1024]{1,0:T(8,128)(2,1)S(1)}, bf16[64,1024]{1,0:T(8,128)(2,1)S(1)}, bf16[64,1024]{1,0:T(8,128)(2...) custom-call(s32[5]{0:T(128)S(1)} %copy-done.3, f32[32,1,128]{2,1,0:T(1,128)S(1)} %all_to_all.11.figures_ref, ...), custom_call_target="tpu_custom_call" | custom-call | tf_op jit(solution)/shard_map/pallas_call | solution.py:227
  134.3 0.6 collective-permute-start.3
  134.8 0.5 collective-permute-start.10
  135.4 0.6 collective-permute-start.6
  136.0 0.5 collective-permute-start.4
  136.5 4.1 %collective-permute-done.3.refs_1_ = bf16[64,1024]{1,0:T(8,128)(2,1)S(1)} collective-permute-done((bf16[64,1024]{1,0:T(8,128)(2,1)S(1)}, bf16[64,1024]{1,0:T(8,128)(2,1)S(1)}, u32[]{:S(2)}, u32[]{:S(2)}) %collective-permute-start.3) | collective-permute-done | bytes 131104 | tf_op jit(solution)/shard_map/ppermute | solution.py:238
  140.6 0.5 collective-permute-start.7
  141.1 0.2 collective-permute-start.5
  141.2 0.0 collective-permute-done.10.refs_8_
  141.2 0.0 collective-permute-done.6.refs_4_
  141.2 1.5 collective-permute-start.8
  142.7 0.5 collective-permute-start.11
  143.3 4.7 %collective-permute-done.4.refs_2_ = bf16[64,1024]{1,0:T(8,128)(2,1)S(1)} collective-permute-done((bf16[64,1024]{1,0:T(8,128)(2,1)S(1)}, bf16[64,1024]{1,0:T(8,128)(2,1)S(1)}, u32[]{:S(2)}, u32[]{:S(2)}) %collective-permute-start.4) | collective-permute-done | bytes 131104 | tf_op jit(solution)/shard_map/ppermute | solution.py:238
  148.0 0.0 collective-permute-done.7.refs_5_
  148.0 1.4 collective-permute-start.14
  149.4 0.0 collective-permute-done.8.refs_12_
  149.4 0.0 collective-permute-done.11.refs_9_
  149.4 1.5 collective-permute-start.12
  150.9 0.5 collective-permute-start.9
  151.4 0.0 collective-permute-done.5.refs_3_
  151.4 2.9 %collective-permute-done.14.refs_10_ = bf16[64,1024]{1,0:T(8,128)(2,1)S(1)} collective-permute-done((bf16[64,1024]{1,0:T(8,128)(2,1)S(1)}, bf16[64,1024]{1,0:T(8,128)(2,1)S(1)}, u32[]{:S(2)}, u32[]{:S(2)}) %collective-permute-start.14) | collective-permute-done | bytes 131104 | tf_op jit(solution)/shard_map/ppermute | solution.py:238
  154.4 1.4 collective-permute-start.15
  155.8 0.0 collective-permute-done.12.refs_13_
  155.8 1.5 collective-permute-start.13
  157.2 0.0 collective-permute-done.9.refs_6_
  157.2 0.2 collective-permute-start.16
  157.5 1.9 %collective-permute-done.15.refs_11_ = bf16[64,1024]{1,0:T(8,128)(2,1)S(1)} collective-permute-done((bf16[64,1024]{1,0:T(8,128)(2,1)S(1)}, bf16[64,1024]{1,0:T(8,128)(2,1)S(1)}, u32[]{:S(2)}, u32[]{:S(2)}) %collective-permute-start.15) | collective-permute-done | bytes 131104 | tf_op jit(solution)/shard_map/ppermute | solution.py:238
  159.4 0.8 collective-permute-start.17
  160.2 0.6 collective-permute-done.13.refs_7_
  160.7 1.5 collective-permute-done.16.refs_14_
  162.2 2.1 %collective-permute-done.17.refs_15_ = bf16[64,1024]{1,0:T(8,128)(2,1)S(1)} collective-permute-done((bf16[64,1024]{1,0:T(8,128)(2,1)S(1)}, bf16[64,1024]{1,0:T(8,128)(2,1)S(1)}, u32[]{:S(2)}, u32[]{:S(2)}) %collective-permute-start.17) | collective-permute-done | bytes 131104 | tf_op jit(solution)/shard_map/ppermute | solution.py:238
  164.3 10.2 %shard_map.113 = (bf16[64,1024]{1,0:T(8,128)(2,1)S(1)}, bf16[64,1024]{1,0:T(8,128)(2,1)S(1)}, bf16[64,1024]{1,0:T(8,128)(2,1)S(1)}, bf16[64,1024]{1,0:T(8,128)(2,1)S(1)}) custom-call(bf16[64,1024]{1,0:T(8,128)(2,1)S(1)} %get-tuple-element.38.refs_0_, bf16[64,1024]{1,0:T(8,128)(2,1)S(1)} %collective-permute-done.3.refs_1_, ...), custom_call_target="tpu_custom_call" | custom-call | tf_op jit(solution)/shard_map/pallas_call | solution.py:85
  174.5 0.1 collective-permute-start.18
  174.6 2.5 %collective-permute-start.19 = (bf16[64,1024]{1,0:T(8,128)(2,1)S(1)}, bf16[64,1024]{1,0:T(8,128)(2,1)S(1)}, u32[]{:S(2)}, u32[]{:S(2)}) collective-permute-start(bf16[64,1024]{1,0:T(8,128)(2,1)S(1)} %get-tuple-element.49), channel_id=1, source_target_pairs={{0,16},{8,24},{16,0},{24,8},{1,17},{9,25},{17,1},{25,9},{2,18},{10... | collective-permute-start | bytes 393224 | tf_op jit(solution)/shard_map/ppermute | solution.py:238
  177.1 1.8 collective-permute-start.20
  179.0 0.0 copy-done.4
  179.0 0.0 copy-done.5
  179.0 0.0 copy-done.6
  179.0 1.4 shard_map.115
  180.4 0.6 collective-permute-done.18.refs_1_
  180.9 0.0 collective-permute-done.19.refs_2_
  180.9 3.0 %collective-permute-done.20.refs_3_ = bf16[64,1024]{1,0:T(8,128)(2,1)S(1)} collective-permute-done((bf16[64,1024]{1,0:T(8,128)(2,1)S(1)}, bf16[64,1024]{1,0:T(8,128)(2,1)S(1)}, u32[]{:S(2)}, u32[]{:S(2)}) %collective-permute-start.20) | collective-permute-done | bytes 131104 | tf_op jit(solution)/shard_map/ppermute | solution.py:238
  184.0 0.0 copy-done.1
  184.0 1.6 shard_map.114
  (4 shorter events, 0.0 us)
Async XLA Ops:
  0.6 71.7 %copy-start.7 = (bf16[1,1,4,256]{3,2,1,0:T(4,128)(2,1)S(1)}, bf16[1,1,4,256]{3,2,1,0:T(4,128)(2,1)}, u32[]{:S(2)}) copy-start(bf16[1,1,4,256]{3,2,1,0:T(4,128)(2,1)} %param.8) | copy-start | bytes 6148
  0.6 117.5 %copy-start = (f32[1,4,64,1024]{3,2,1,0:T(8,128)S(1)}, f32[1,4,64,1024]{3,2,1,0:T(8,128)}, u32[]{:S(2)}) copy-start(f32[1,4,64,1024]{3,2,1,0:T(8,128)} %param.9) | copy-start | bytes 3145732
  1.2 117.0 %copy-start.3 = (s32[5]{0:T(128)S(1)}, s32[5]{0:T(128)}, u32[]{:S(2)}) copy-start(s32[5]{0:T(128)} %compare_select_fusion.place_ref) | copy-start | bytes 64
  66.6 51.5 %collective-permute-start = (bf16[4,64,1024]{2,1,0:T(8,128)(2,1)}, bf16[4,64,1024]{2,1,0:T(8,128)(2,1)S(1)}, u32[]{:S(2)}, u32[]{:S(2)}) collective-permute-start(bf16[4,64,1024]{2,1,0:T(8,128)(2,1)} %get-tuple-element.32), channel_id=1, source_target_pairs={{0,8},{8,0},{16,24},{24,16},{1,9},{9,1},{17,25},{25,17},{2,10},{10... | collective-permute-start | bytes 1572872 | tf_op jit(solution)/shard_map/ppermute | solution.py:238
  69.7 48.4 %collective-permute-start.1 = (bf16[4,64,1024]{2,1,0:T(8,128)(2,1)}, bf16[4,64,1024]{2,1,0:T(8,128)(2,1)S(1)}, u32[]{:S(2)}, u32[]{:S(2)}) collective-permute-start(bf16[4,64,1024]{2,1,0:T(8,128)(2,1)} %get-tuple-element.33), channel_id=1, source_target_pairs={{0,16},{8,24},{16,0},{24,8},{1,17},{9,25},{17,1},{25,9},{2,18},{10... | collective-permute-start | bytes 1572872 | tf_op jit(solution)/shard_map/ppermute | solution.py:238
  72.3 45.8 %collective-permute-start.2 = (bf16[4,64,1024]{2,1,0:T(8,128)(2,1)}, bf16[4,64,1024]{2,1,0:T(8,128)(2,1)S(1)}, u32[]{:S(2)}, u32[]{:S(2)}) collective-permute-start(bf16[4,64,1024]{2,1,0:T(8,128)(2,1)} %get-tuple-element.34), channel_id=1, source_target_pairs={{0,24},{8,16},{16,8},{24,0},{1,25},{9,17},{17,9},{25,1},{2,26},{10... | collective-permute-start | bytes 1572872 | tf_op jit(solution)/shard_map/ppermute | solution.py:238
  118.2 1.0 copy-start.2
  132.3 46.7 %copy-start.4 = (f32[1,4,64]{2,1,0:T(4,128)S(1)}, f32[1,4,64]{2,1,0:T(4,128)}, u32[]{:S(2)}) copy-start(f32[1,4,64]{2,1,0:T(4,128)} %param.11) | copy-start | bytes 3076
  132.3 46.7 %copy-start.5 = (f32[1,4,64]{2,1,0:T(4,128)S(1)}, f32[1,4,64]{2,1,0:T(4,128)}, u32[]{:S(2)}) copy-start(f32[1,4,64]{2,1,0:T(4,128)} %param.12) | copy-start | bytes 3076
  132.3 46.7 %copy-start.6 = (f32[1,4,64]{2,1,0:T(4,128)S(1)}, f32[1,4,64]{2,1,0:T(4,128)}, u32[]{:S(2)}) copy-start(f32[1,4,64]{2,1,0:T(4,128)} %param.13) | copy-start | bytes 3076
  132.3 51.7 %copy-start.1 = (bf16[1,4,64,1024]{3,2,1,0:T(8,128)(2,1)S(1)}, bf16[1,4,64,1024]{3,2,1,0:T(8,128)(2,1)}, u32[]{:S(2)}) copy-start(bf16[1,4,64,1024]{3,2,1,0:T(8,128)(2,1)} %param.10) | copy-start | bytes 1572868
  134.3 6.3 %collective-permute-start.3 = (bf16[64,1024]{1,0:T(8,128)(2,1)S(1)}, bf16[64,1024]{1,0:T(8,128)(2,1)S(1)}, u32[]{:S(2)}, u32[]{:S(2)}) collective-permute-start(bf16[64,1024]{1,0:T(8,128)(2,1)S(1)} %get-tuple-element.39), channel_id=1, source_target_pairs={{0,8},{8,0},{16,24},{24,16},{1,9},{9,1},{17,25},{25,17},{2,10},{10... | collective-permute-start | bytes 393224 | tf_op jit(solution)/shard_map/ppermute | solution.py:238
  134.8 6.4 %collective-permute-start.10 = (bf16[64,1024]{1,0:T(8,128)(2,1)S(1)}, bf16[64,1024]{1,0:T(8,128)(2,1)S(1)}, u32[]{:S(2)}, u32[]{:S(2)}) collective-permute-start(bf16[64,1024]{1,0:T(8,128)(2,1)S(1)} %get-tuple-element.38.refs_0_), channel_id=1, source_target_pairs={{0,4},{2,6},{4,0},{6,2},{1,5},{3,7},{5,1},{7,3},{8,12},{10,14},{12... | collective-permute-start | bytes 393224 | tf_op jit(solution)/shard_map/ppermute | solution.py:238
  135.4 5.8 %collective-permute-start.6 = (bf16[64,1024]{1,0:T(8,128)(2,1)S(1)}, bf16[64,1024]{1,0:T(8,128)(2,1)S(1)}, u32[]{:S(2)}, u32[]{:S(2)}) collective-permute-start(bf16[64,1024]{1,0:T(8,128)(2,1)S(1)} %get-tuple-element.38.refs_0_), channel_id=1, source_target_pairs={{0,2},{2,0},{4,6},{6,4},{1,3},{3,1},{5,7},{7,5},{8,10},{10,8},{12,... | collective-permute-start | bytes 393224 | tf_op jit(solution)/shard_map/ppermute | solution.py:238
  136.0 12.0 %collective-permute-start.4 = (bf16[64,1024]{1,0:T(8,128)(2,1)S(1)}, bf16[64,1024]{1,0:T(8,128)(2,1)S(1)}, u32[]{:S(2)}, u32[]{:S(2)}) collective-permute-start(bf16[64,1024]{1,0:T(8,128)(2,1)S(1)} %get-tuple-element.40), channel_id=1, source_target_pairs={{0,16},{8,24},{16,0},{24,8},{1,17},{9,25},{17,1},{25,9},{2,18},{10... | collective-permute-start | bytes 393224 | tf_op jit(solution)/shard_map/ppermute | solution.py:238
  140.6 7.4 %collective-permute-start.7 = (bf16[64,1024]{1,0:T(8,128)(2,1)S(1)}, bf16[64,1024]{1,0:T(8,128)(2,1)S(1)}, u32[]{:S(2)}, u32[]{:S(2)}) collective-permute-start(bf16[64,1024]{1,0:T(8,128)(2,1)S(1)} %collective-permute-done.3.refs_1_), channel_id=1, source_target_pairs={{0,2},{2,0},{4,6},{6,4},{1,3},{3,1},{5,7},{7,5},{8,10},{10,8},{12,... | collective-permute-start | bytes 393224 | tf_op jit(solution)/shard_map/ppermute | solution.py:238
  141.1 10.4 %collective-permute-start.5 = (bf16[64,1024]{1,0:T(8,128)(2,1)S(1)}, bf16[64,1024]{1,0:T(8,128)(2,1)S(1)}, u32[]{:S(2)}, u32[]{:S(2)}) collective-permute-start(bf16[64,1024]{1,0:T(8,128)(2,1)S(1)} %get-tuple-element.41), channel_id=1, source_target_pairs={{0,24},{8,16},{16,8},{24,0},{1,25},{9,17},{17,9},{25,1},{2,26},{10... | collective-permute-start | bytes 393224 | tf_op jit(solution)/shard_map/ppermute | solution.py:238
  141.2 8.2 %collective-permute-start.8 = (bf16[64,1024]{1,0:T(8,128)(2,1)S(1)}, bf16[64,1024]{1,0:T(8,128)(2,1)S(1)}, u32[]{:S(2)}, u32[]{:S(2)}) collective-permute-start(bf16[64,1024]{1,0:T(8,128)(2,1)S(1)} %collective-permute-done.6.refs_4_), channel_id=1, source_target_pairs={{0,4},{2,6},{4,0},{6,2},{1,5},{3,7},{5,1},{7,3},{8,12},{10,14},{12... | collective-permute-start | bytes 393224 | tf_op jit(solution)/shard_map/ppermute | solution.py:238
  142.7 6.7 %collective-permute-start.11 = (bf16[64,1024]{1,0:T(8,128)(2,1)S(1)}, bf16[64,1024]{1,0:T(8,128)(2,1)S(1)}, u32[]{:S(2)}, u32[]{:S(2)}) collective-permute-start(bf16[64,1024]{1,0:T(8,128)(2,1)S(1)} %collective-permute-done.3.refs_1_), channel_id=1, source_target_pairs={{0,4},{2,6},{4,0},{6,2},{1,5},{3,7},{5,1},{7,3},{8,12},{10,14},{12... | collective-permute-start | bytes 393224 | tf_op jit(solution)/shard_map/ppermute | solution.py:238
  148.0 6.4 %collective-permute-start.14 = (bf16[64,1024]{1,0:T(8,128)(2,1)S(1)}, bf16[64,1024]{1,0:T(8,128)(2,1)S(1)}, u32[]{:S(2)}, u32[]{:S(2)}) collective-permute-start(bf16[64,1024]{1,0:T(8,128)(2,1)S(1)} %collective-permute-done.4.refs_2_), channel_id=1, source_target_pairs={{0,4},{2,6},{4,0},{6,2},{1,5},{3,7},{5,1},{7,3},{8,12},{10,14},{12... | collective-permute-start | bytes 393224 | tf_op jit(solution)/shard_map/ppermute | solution.py:238
  149.4 6.4 %collective-permute-start.12 = (bf16[64,1024]{1,0:T(8,128)(2,1)S(1)}, bf16[64,1024]{1,0:T(8,128)(2,1)S(1)}, u32[]{:S(2)}, u32[]{:S(2)}) collective-permute-start(bf16[64,1024]{1,0:T(8,128)(2,1)S(1)} %collective-permute-done.11.refs_9_), channel_id=1, source_target_pairs={{0,2},{2,0},{4,6},{6,4},{1,3},{3,1},{5,7},{7,5},{8,10},{10,8},{12,... | collective-permute-start | bytes 393224 | tf_op jit(solution)/shard_map/ppermute | solution.py:238
  150.9 6.3 %collective-permute-start.9 = (bf16[64,1024]{1,0:T(8,128)(2,1)S(1)}, bf16[64,1024]{1,0:T(8,128)(2,1)S(1)}, u32[]{:S(2)}, u32[]{:S(2)}) collective-permute-start(bf16[64,1024]{1,0:T(8,128)(2,1)S(1)} %collective-permute-done.4.refs_2_), channel_id=1, source_target_pairs={{0,2},{2,0},{4,6},{6,4},{1,3},{3,1},{5,7},{7,5},{8,10},{10,8},{12,... | collective-permute-start | bytes 393224 | tf_op jit(solution)/shard_map/ppermute | solution.py:238
  154.4 5.0 %collective-permute-start.15 = (bf16[64,1024]{1,0:T(8,128)(2,1)S(1)}, bf16[64,1024]{1,0:T(8,128)(2,1)S(1)}, u32[]{:S(2)}, u32[]{:S(2)}) collective-permute-start(bf16[64,1024]{1,0:T(8,128)(2,1)S(1)} %collective-permute-done.5.refs_3_), channel_id=1, source_target_pairs={{0,4},{2,6},{4,0},{6,2},{1,5},{3,7},{5,1},{7,3},{8,12},{10,14},{12... | collective-permute-start | bytes 393224 | tf_op jit(solution)/shard_map/ppermute | solution.py:238
  155.8 5.0 %collective-permute-start.13 = (bf16[64,1024]{1,0:T(8,128)(2,1)S(1)}, bf16[64,1024]{1,0:T(8,128)(2,1)S(1)}, u32[]{:S(2)}, u32[]{:S(2)}) collective-permute-start(bf16[64,1024]{1,0:T(8,128)(2,1)S(1)} %collective-permute-done.5.refs_3_), channel_id=1, source_target_pairs={{0,2},{2,0},{4,6},{6,4},{1,3},{3,1},{5,7},{7,5},{8,10},{10,8},{12,... | collective-permute-start | bytes 393224 | tf_op jit(solution)/shard_map/ppermute | solution.py:238
  157.2 5.0 %collective-permute-start.16 = (bf16[64,1024]{1,0:T(8,128)(2,1)S(1)}, bf16[64,1024]{1,0:T(8,128)(2,1)S(1)}, u32[]{:S(2)}, u32[]{:S(2)}) collective-permute-start(bf16[64,1024]{1,0:T(8,128)(2,1)S(1)} %collective-permute-done.9.refs_6_), channel_id=1, source_target_pairs={{0,4},{2,6},{4,0},{6,2},{1,5},{3,7},{5,1},{7,3},{8,12},{10,14},{12... | collective-permute-start | bytes 393224 | tf_op jit(solution)/shard_map/ppermute | solution.py:238
  159.4 5.0 %collective-permute-start.17 = (bf16[64,1024]{1,0:T(8,128)(2,1)S(1)}, bf16[64,1024]{1,0:T(8,128)(2,1)S(1)}, u32[]{:S(2)}, u32[]{:S(2)}) collective-permute-start(bf16[64,1024]{1,0:T(8,128)(2,1)S(1)} %collective-permute-done.15.refs_11_), channel_id=1, source_target_pairs={{0,2},{2,0},{4,6},{6,4},{1,3},{3,1},{5,7},{7,5},{8,10},{10,8},{12,... | collective-permute-start | bytes 393224 | tf_op jit(solution)/shard_map/ppermute | solution.py:238
  174.5 6.4 %collective-permute-start.18 = (bf16[64,1024]{1,0:T(8,128)(2,1)S(1)}, bf16[64,1024]{1,0:T(8,128)(2,1)S(1)}, u32[]{:S(2)}, u32[]{:S(2)}) collective-permute-start(bf16[64,1024]{1,0:T(8,128)(2,1)S(1)} %get-tuple-element.48), channel_id=1, source_target_pairs={{0,8},{8,0},{16,24},{24,16},{1,9},{9,1},{17,25},{25,17},{2,10},{10... | collective-permute-start | bytes 393224 | tf_op jit(solution)/shard_map/ppermute | solution.py:238
  174.6 6.4 %collective-permute-start.19 = (bf16[64,1024]{1,0:T(8,128)(2,1)S(1)}, bf16[64,1024]{1,0:T(8,128)(2,1)S(1)}, u32[]{:S(2)}, u32[]{:S(2)}) collective-permute-start(bf16[64,1024]{1,0:T(8,128)(2,1)S(1)} %get-tuple-element.49), channel_id=1, source_target_pairs={{0,16},{8,24},{16,0},{24,8},{1,17},{9,25},{17,1},{25,9},{2,18},{10... | collective-permute-start | bytes 393224 | tf_op jit(solution)/shard_map/ppermute | solution.py:238
  177.1 6.9 %collective-permute-start.20 = (bf16[64,1024]{1,0:T(8,128)(2,1)S(1)}, bf16[64,1024]{1,0:T(8,128)(2,1)S(1)}, u32[]{:S(2)}, u32[]{:S(2)}) collective-permute-start(bf16[64,1024]{1,0:T(8,128)(2,1)S(1)} %get-tuple-element.50), channel_id=1, source_target_pairs={{0,24},{8,16},{16,8},{24,0},{1,25},{9,17},{17,9},{25,1},{2,26},{10... | collective-permute-start | bytes 393224 | tf_op jit(solution)/shard_map/ppermute | solution.py:238

commit v3 on v2

--- a/solution.py
+++ b/solution.py
@@ -126,7 +126,7 @@
             pl.BlockSpec(memory_space=pltpu.SMEM),
             pl.BlockSpec(memory_space=pltpu.HBM),
         ],
-        out_specs=[pl.BlockSpec(memory_space=pltpu.HBM)] * shard_count,
+        out_specs=[pl.BlockSpec(memory_space=pltpu.VMEM)] * shard_count,
         scratch_shapes=[pltpu.SemaphoreType.DMA((shard_count,))],
     )(place, by_rows)
 

time: 186 us -> 124 us (0.67)
  Pallas kernels: 82 us -> 20.2 us
    pallas_call x1, Pallas kernels: 65.5 us -> 3.66 us  [row_slices(): pl.pallas_call(functools.partial(slices_kernel, shard_count), out_shape=[...]
where the time goes in v3:
time: 124 us
  blocking collectives  57.5 us (46%)
  starting transfers between devices  22.4 us (18%)
  waiting for transfers between devices  21.4 us (17%)
  Pallas kernels  20.2 us (16%)
    all_to_all x1, blocking collectives, per_device(): lax.all_to_all(jnp.broadcast_to(vector_grads[0], (shard_count, vector_cou...  45.8 us
    ppermute x21, starting transfers between devices, swapped(): return lax.ppermute(array, axis, pairs)  22.4 us
    ppermute x21, waiting for transfers between devices, swapped(): return lax.ppermute(array, axis, pairs)  21.4 us
    all_to_all x1, blocking collectives, per_device(): lax.all_to_all(figures.reshape(others * section_count, 1, LANES), MESH_AX...  11.7 us
    pallas_call x1, Pallas kernels, orthogonalize(): pl.pallas_call(functools.partial(orthogonalize_kernel, count, pieces), ou...  10.2 us
    pallas_call x4, Pallas kernels, on_device(): pl.pallas_call(kernel, out_shape=out_shape, in_specs=[pl.BlockSpec(memory...  6.39 us
    pallas_call x1, Pallas kernels, row_slices(): pl.pallas_call(functools.partial(slices_kernel, shard_count), out_shape=[...  3.66 us
  transfers between devices with their start and end apart: 21, of which 9 were waited for; matrix products, arithmetic and copies ran while one was open for 0% of the time, Pallas kernels for 1%

profile of v3, /device:TPU:0, one launch (start us, length us, event | category | flops | bytes accessed | tf_op | source)
XLA Modules:
  0.0 123.8 jit_solution(2991801616540761064)
XLA Ops:
  0.6 0.0 copy-start.7
  0.6 0.0 copy-start
  0.7 0.5 compare_select_fusion.place_ref
  1.2 0.0 copy-start.3
  1.2 3.7 %shard_map.110 = (bf16[4,64,1024]{2,1,0:T(8,128)(2,1)}, bf16[4,64,1024]{2,1,0:T(8,128)(2,1)}, bf16[4,64,1024]{2,1,0:T(8,128)(2,1)}, bf16[4,64,1024]{2,1,0:T(8,128)(2,1)}) custom-call(s32[5]{0:T(128)} %compare_select_fusion.place_ref, bf16[4,4,64,1024]{3,2,1,0:T(8,128)(2,1)} %bitcast.20), custom_call_target="tpu_custom_call" | custom-call | tf_op jit(solution)/shard_map/pallas_call | solution.py:121
  4.8 3.1 %collective-permute-start = (bf16[4,64,1024]{2,1,0:T(8,128)(2,1)}, bf16[4,64,1024]{2,1,0:T(8,128)(2,1)S(1)}, u32[]{:S(2)}, u32[]{:S(2)}) collective-permute-start(bf16[4,64,1024]{2,1,0:T(8,128)(2,1)} %get-tuple-element.32), channel_id=1, source_target_pairs={{0,8},{8,0},{16,24},{24,16},{1,9},{9,1},{17,25},{25,17},{2,10},{10... | collective-permute-start | bytes 1572872 | tf_op jit(solution)/shard_map/ppermute | solution.py:238
  7.9 2.6 %collective-permute-start.1 = (bf16[4,64,1024]{2,1,0:T(8,128)(2,1)}, bf16[4,64,1024]{2,1,0:T(8,128)(2,1)S(1)}, u32[]{:S(2)}, u32[]{:S(2)}) collective-permute-start(bf16[4,64,1024]{2,1,0:T(8,128)(2,1)} %get-tuple-element.33), channel_id=1, source_target_pairs={{0,16},{8,24},{16,0},{24,8},{1,17},{9,25},{17,1},{25,9},{2,18},{10... | collective-permute-start | bytes 1572872 | tf_op jit(solution)/shard_map/ppermute | solution.py:238
  10.5 0.0 collective-permute-start.2
  10.5 0.0 copy-done.7
  10.5 45.8 %all_to_all.10.refs_4_ = bf16[4,4,256]{2,1,0:T(4,128)(2,1)S(1)} all-to-all(bf16[4,4,256]{2,1,0:T(4,128)(2,1)S(1)} %broadcast_in_dim.28), channel_id=1, replica_groups=mesh['shard'=4,'tensor'=4,'section'=2] {'shard'}, dimensions={0} | all-to-all | bytes 16384 | tf_op jit(solution)/shard_map/all_to_all | solution.py:267
  56.4 0.0 collective-permute-done.refs_1_
  56.4 0.0 collective-permute-done.1.refs_2_
  56.4 0.0 collective-permute-done.2.refs_3_
  56.4 0.0 copy-done
  56.4 0.0 copy-done.3
  56.4 0.0 copy-start.2
  56.4 1.0 copy-done.2
  57.4 1.3 %shard_map.111 = (f32[4,64,1024]{2,1,0:T(8,128)S(1)}, f32[4,256]{1,0:T(4,128)S(1)}, f32[16,2,1,128]{3,2,1,0:T(1,128)S(1)}) custom-call(s32[5]{0:T(128)S(1)} %copy-done.3, bf16[4,64,1024]{2,1,0:T(8,128)(2,1)S(1)} %copy-done.2, bf16[4,64,1024]{2,1,0:T(8,128)(2,1)S(1)} %collective-permute-done.refs_1_, bf16[4,64,1024]{2,1,0:T(8,128)(2,1)S(1)} %collective-permute-done.1.refs_2_, ...), custom_call_target="tpu_custom_call" | custom-call | tf_op jit(solution)/shard_map/pallas_call | solution.py:227
  58.8 11.7 %all_to_all.11.figures_ref = f32[32,1,128]{2,1,0:T(1,128)S(1)} all-to-all(f32[32,1,128]{2,1,0:T(1,128)S(1)} %bitcast.16), channel_id=1, replica_groups=mesh['shard'=4,'tensor'=4,'section'=2] {'shard','tensor','section'}, dimensions={0} | all-to-all | bytes 32768 | tf_op jit(solution)/shard_map/all_to_all | solution.py:286
  70.5 0.0 copy-start.4
  70.5 2.0 %shard_map.112 = (bf16[64,1024]{1,0:T(8,128)(2,1)S(1)}, bf16[64,1024]{1,0:T(8,128)(2,1)S(1)}, bf16[64,1024]{1,0:T(8,128)(2,1)S(1)}, bf16[64,1024]{1,0:T(8,128)(2...) custom-call(s32[5]{0:T(128)S(1)} %copy-done.3, f32[32,1,128]{2,1,0:T(1,128)S(1)} %all_to_all.11.figures_ref, ...), custom_call_target="tpu_custom_call" | custom-call | tf_op jit(solution)/shard_map/pallas_call | solution.py:227
  72.5 0.6 collective-permute-start.3
  73.0 0.5 collective-permute-start.10
  73.6 0.6 collective-permute-start.6
  74.2 0.5 collective-permute-start.4
  74.7 4.1 %collective-permute-done.3.refs_1_ = bf16[64,1024]{1,0:T(8,128)(2,1)S(1)} collective-permute-done((bf16[64,1024]{1,0:T(8,128)(2,1)S(1)}, bf16[64,1024]{1,0:T(8,128)(2,1)S(1)}, u32[]{:S(2)}, u32[]{:S(2)}) %collective-permute-start.3) | collective-permute-done | bytes 131104 | tf_op jit(solution)/shard_map/ppermute | solution.py:238
  78.8 0.5 collective-permute-start.7
  79.3 0.2 collective-permute-start.5
  79.4 0.0 collective-permute-done.10.refs_8_
  79.4 0.0 collective-permute-done.6.refs_4_
  79.4 1.5 %collective-permute-start.8 = (bf16[64,1024]{1,0:T(8,128)(2,1)S(1)}, bf16[64,1024]{1,0:T(8,128)(2,1)S(1)}, u32[]{:S(2)}, u32[]{:S(2)}) collective-permute-start(bf16[64,1024]{1,0:T(8,128)(2,1)S(1)} %collective-permute-done.6.refs_4_), channel_id=1, source_target_pairs={{0,4},{2,6},{4,0},{6,2},{1,5},{3,7},{5,1},{7,3},{8,12},{10,14},{12... | collective-permute-start | bytes 393224 | tf_op jit(solution)/shard_map/ppermute | solution.py:238
  80.9 0.5 collective-permute-start.11
  81.5 4.7 %collective-permute-done.4.refs_2_ = bf16[64,1024]{1,0:T(8,128)(2,1)S(1)} collective-permute-done((bf16[64,1024]{1,0:T(8,128)(2,1)S(1)}, bf16[64,1024]{1,0:T(8,128)(2,1)S(1)}, u32[]{:S(2)}, u32[]{:S(2)}) %collective-permute-start.4) | collective-permute-done | bytes 131104 | tf_op jit(solution)/shard_map/ppermute | solution.py:238
  86.2 0.0 collective-permute-done.7.refs_5_
  86.2 1.4 %collective-permute-start.14 = (bf16[64,1024]{1,0:T(8,128)(2,1)S(1)}, bf16[64,1024]{1,0:T(8,128)(2,1)S(1)}, u32[]{:S(2)}, u32[]{:S(2)}) collective-permute-start(bf16[64,1024]{1,0:T(8,128)(2,1)S(1)} %collective-permute-done.4.refs_2_), channel_id=1, source_target_pairs={{0,4},{2,6},{4,0},{6,2},{1,5},{3,7},{5,1},{7,3},{8,12},{10,14},{12... | collective-permute-start | bytes 393224 | tf_op jit(solution)/shard_map/ppermute | solution.py:238
  87.6 0.0 collective-permute-done.8.refs_12_
  87.6 0.0 collective-permute-done.11.refs_9_
  87.6 1.5 %collective-permute-start.12 = (bf16[64,1024]{1,0:T(8,128)(2,1)S(1)}, bf16[64,1024]{1,0:T(8,128)(2,1)S(1)}, u32[]{:S(2)}, u32[]{:S(2)}) collective-permute-start(bf16[64,1024]{1,0:T(8,128)(2,1)S(1)} %collective-permute-done.11.refs_9_), channel_id=1, source_target_pairs={{0,2},{2,0},{4,6},{6,4},{1,3},{3,1},{5,7},{7,5},{8,10},{10,8},{12,... | collective-permute-start | bytes 393224 | tf_op jit(solution)/shard_map/ppermute | solution.py:238
  89.1 0.5 collective-permute-start.9
  89.6 0.0 collective-permute-done.5.refs_3_
  89.6 2.9 %collective-permute-done.14.refs_10_ = bf16[64,1024]{1,0:T(8,128)(2,1)S(1)} collective-permute-done((bf16[64,1024]{1,0:T(8,128)(2,1)S(1)}, bf16[64,1024]{1,0:T(8,128)(2,1)S(1)}, u32[]{:S(2)}, u32[]{:S(2)}) %collective-permute-start.14) | collective-permute-done | bytes 131104 | tf_op jit(solution)/shard_map/ppermute | solution.py:238
  92.6 1.4 %collective-permute-start.15 = (bf16[64,1024]{1,0:T(8,128)(2,1)S(1)}, bf16[64,1024]{1,0:T(8,128)(2,1)S(1)}, u32[]{:S(2)}, u32[]{:S(2)}) collective-permute-start(bf16[64,1024]{1,0:T(8,128)(2,1)S(1)} %collective-permute-done.5.refs_3_), channel_id=1, source_target_pairs={{0,4},{2,6},{4,0},{6,2},{1,5},{3,7},{5,1},{7,3},{8,12},{10,14},{12... | collective-permute-start | bytes 393224 | tf_op jit(solution)/shard_map/ppermute | solution.py:238
  94.0 0.0 collective-permute-done.12.refs_13_
  94.0 1.5 %collective-permute-start.13 = (bf16[64,1024]{1,0:T(8,128)(2,1)S(1)}, bf16[64,1024]{1,0:T(8,128)(2,1)S(1)}, u32[]{:S(2)}, u32[]{:S(2)}) collective-permute-start(bf16[64,1024]{1,0:T(8,128)(2,1)S(1)} %collective-permute-done.5.refs_3_), channel_id=1, source_target_pairs={{0,2},{2,0},{4,6},{6,4},{1,3},{3,1},{5,7},{7,5},{8,10},{10,8},{12,... | collective-permute-start | bytes 393224 | tf_op jit(solution)/shard_map/ppermute | solution.py:238
  95.4 0.0 collective-permute-done.9.refs_6_
  95.4 0.2 collective-permute-start.16
  95.7 1.9 %collective-permute-done.15.refs_11_ = bf16[64,1024]{1,0:T(8,128)(2,1)S(1)} collective-permute-done((bf16[64,1024]{1,0:T(8,128)(2,1)S(1)}, bf16[64,1024]{1,0:T(8,128)(2,1)S(1)}, u32[]{:S(2)}, u32[]{:S(2)}) %collective-permute-start.15) | collective-permute-done | bytes 131104 | tf_op jit(solution)/shard_map/ppermute | solution.py:238
  97.5 0.8 collective-permute-start.17
  98.4 0.6 collective-permute-done.13.refs_7_
  98.9 1.5 %collective-permute-done.16.refs_14_ = bf16[64,1024]{1,0:T(8,128)(2,1)S(1)} collective-permute-done((bf16[64,1024]{1,0:T(8,128)(2,1)S(1)}, bf16[64,1024]{1,0:T(8,128)(2,1)S(1)}, u32[]{:S(2)}, u32[]{:S(2)}) %collective-permute-start.16) | collective-permute-done | bytes 131104 | tf_op jit(solution)/shard_map/ppermute | solution.py:238
  100.4 2.1 %collective-permute-done.17.refs_15_ = bf16[64,1024]{1,0:T(8,128)(2,1)S(1)} collective-permute-done((bf16[64,1024]{1,0:T(8,128)(2,1)S(1)}, bf16[64,1024]{1,0:T(8,128)(2,1)S(1)}, u32[]{:S(2)}, u32[]{:S(2)}) %collective-permute-start.17) | collective-permute-done | bytes 131104 | tf_op jit(solution)/shard_map/ppermute | solution.py:238
  102.5 10.2 %shard_map.113 = (bf16[64,1024]{1,0:T(8,128)(2,1)S(1)}, bf16[64,1024]{1,0:T(8,128)(2,1)S(1)}, bf16[64,1024]{1,0:T(8,128)(2,1)S(1)}, bf16[64,1024]{1,0:T(8,128)(2,1)S(1)}) custom-call(bf16[64,1024]{1,0:T(8,128)(2,1)S(1)} %get-tuple-element.38.refs_0_, bf16[64,1024]{1,0:T(8,128)(2,1)S(1)} %collective-permute-done.3.refs_1_, ...), custom_call_target="tpu_custom_call" | custom-call | tf_op jit(solution)/shard_map/pallas_call | solution.py:85
  112.7 0.1 collective-permute-start.18
  112.8 2.5 %collective-permute-start.19 = (bf16[64,1024]{1,0:T(8,128)(2,1)S(1)}, bf16[64,1024]{1,0:T(8,128)(2,1)S(1)}, u32[]{:S(2)}, u32[]{:S(2)}) collective-permute-start(bf16[64,1024]{1,0:T(8,128)(2,1)S(1)} %get-tuple-element.49), channel_id=1, source_target_pairs={{0,16},{8,24},{16,0},{24,8},{1,17},{9,25},{17,1},{25,9},{2,18},{10... | collective-permute-start | bytes 393224 | tf_op jit(solution)/shard_map/ppermute | solution.py:238
  115.3 1.8 %collective-permute-start.20 = (bf16[64,1024]{1,0:T(8,128)(2,1)S(1)}, bf16[64,1024]{1,0:T(8,128)(2,1)S(1)}, u32[]{:S(2)}, u32[]{:S(2)}) collective-permute-start(bf16[64,1024]{1,0:T(8,128)(2,1)S(1)} %get-tuple-element.50), channel_id=1, source_target_pairs={{0,24},{8,16},{16,8},{24,0},{1,25},{9,17},{17,9},{25,1},{2,26},{10... | collective-permute-start | bytes 393224 | tf_op jit(solution)/shard_map/ppermute | solution.py:238
  117.2 0.0 copy-done.4
  117.2 0.0 copy-done.5
  117.2 0.0 copy-done.6
  117.2 1.4 %shard_map.115 = (f32[4,64]{1,0:T(4,128)}, f32[4,64]{1,0:T(4,128)}) custom-call(s32[5]{0:T(128)S(1)} %copy-done.3, f32[8,128]{1,0:T(8,128)S(1)} %get-tuple-element.53.clip_ref, f32[4,256]{1,0:T(4,128)S(1)} %get-tuple-element.54.sums_ref, f32[4,64]{1,0:T(4,128)S(1)} %bitcast.17, f32[4,64]{1,0:T(4,128)S(1)} %bitcast.18, f32[4,64]{1,0:T(4,128)S(1)} %bitcast.19), custom_call_target="tpu_custom_call" | custom-call | tf_op jit(solution)/shard_map/pallas_call | solution.py:227
  118.6 0.6 collective-permute-done.18.refs_1_
  119.1 0.0 collective-permute-done.19.refs_2_
  119.1 3.0 %collective-permute-done.20.refs_3_ = bf16[64,1024]{1,0:T(8,128)(2,1)S(1)} collective-permute-done((bf16[64,1024]{1,0:T(8,128)(2,1)S(1)}, bf16[64,1024]{1,0:T(8,128)(2,1)S(1)}, u32[]{:S(2)}, u32[]{:S(2)}) %collective-permute-start.20) | collective-permute-done | bytes 131104 | tf_op jit(solution)/shard_map/ppermute | solution.py:238
  122.2 0.0 copy-done.1
  122.2 1.6 %shard_map.114 = (bf16[4,64,1024]{2,1,0:T(8,128)(2,1)}, bf16[4,64,1024]{2,1,0:T(8,128)(2,1)}) custom-call(s32[5]{0:T(128)S(1)} %copy-done.3, bf16[64,1024]{1,0:T(8,128)(2,1)S(1)} %get-tuple-element.47.refs_0_, bf16[64,1024]{1,0:T(8,128)(2,1)S(1)} %collective-permute-done.18.refs_1_, bf16[64,1024]{1,0:T(8,128)(2,1)S(1)} %collective-permute-done.19.refs_2_, ...), custom_call_target="tpu_custom_call" | custom-call | tf_op jit(solution)/shard_map/pallas_call | solution.py:227
  (4 shorter events, 0.0 us)
Async XLA Ops:
  0.6 9.9 %copy-start.7 = (bf16[1,1,4,256]{3,2,1,0:T(4,128)(2,1)S(1)}, bf16[1,1,4,256]{3,2,1,0:T(4,128)(2,1)}, u32[]{:S(2)}) copy-start(bf16[1,1,4,256]{3,2,1,0:T(4,128)(2,1)} %param.8) | copy-start | bytes 6148
  0.6 55.7 %copy-start = (f32[1,4,64,1024]{3,2,1,0:T(8,128)S(1)}, f32[1,4,64,1024]{3,2,1,0:T(8,128)}, u32[]{:S(2)}) copy-start(f32[1,4,64,1024]{3,2,1,0:T(8,128)} %param.9) | copy-start | bytes 3145732
  1.2 55.2 %copy-start.3 = (s32[5]{0:T(128)S(1)}, s32[5]{0:T(128)}, u32[]{:S(2)}) copy-start(s32[5]{0:T(128)} %compare_select_fusion.place_ref) | copy-start | bytes 64
  4.8 51.5 %collective-permute-start = (bf16[4,64,1024]{2,1,0:T(8,128)(2,1)}, bf16[4,64,1024]{2,1,0:T(8,128)(2,1)S(1)}, u32[]{:S(2)}, u32[]{:S(2)}) collective-permute-start(bf16[4,64,1024]{2,1,0:T(8,128)(2,1)} %get-tuple-element.32), channel_id=1, source_target_pairs={{0,8},{8,0},{16,24},{24,16},{1,9},{9,1},{17,25},{25,17},{2,10},{10... | collective-permute-start | bytes 1572872 | tf_op jit(solution)/shard_map/ppermute | solution.py:238
  7.9 48.4 %collective-permute-start.1 = (bf16[4,64,1024]{2,1,0:T(8,128)(2,1)}, bf16[4,64,1024]{2,1,0:T(8,128)(2,1)S(1)}, u32[]{:S(2)}, u32[]{:S(2)}) collective-permute-start(bf16[4,64,1024]{2,1,0:T(8,128)(2,1)} %get-tuple-element.33), channel_id=1, source_target_pairs={{0,16},{8,24},{16,0},{24,8},{1,17},{9,25},{17,1},{25,9},{2,18},{10... | collective-permute-start | bytes 1572872 | tf_op jit(solution)/shard_map/ppermute | solution.py:238
  10.5 45.8 %collective-permute-start.2 = (bf16[4,64,1024]{2,1,0:T(8,128)(2,1)}, bf16[4,64,1024]{2,1,0:T(8,128)(2,1)S(1)}, u32[]{:S(2)}, u32[]{:S(2)}) collective-permute-start(bf16[4,64,1024]{2,1,0:T(8,128)(2,1)} %get-tuple-element.34), channel_id=1, source_target_pairs={{0,24},{8,16},{16,8},{24,0},{1,25},{9,17},{17,9},{25,1},{2,26},{10... | collective-permute-start | bytes 1572872 | tf_op jit(solution)/shard_map/ppermute | solution.py:238
  56.4 1.0 copy-start.2
  70.5 46.7 %copy-start.4 = (f32[1,4,64]{2,1,0:T(4,128)S(1)}, f32[1,4,64]{2,1,0:T(4,128)}, u32[]{:S(2)}) copy-start(f32[1,4,64]{2,1,0:T(4,128)} %param.11) | copy-start | bytes 3076
  70.5 46.7 %copy-start.5 = (f32[1,4,64]{2,1,0:T(4,128)S(1)}, f32[1,4,64]{2,1,0:T(4,128)}, u32[]{:S(2)}) copy-start(f32[1,4,64]{2,1,0:T(4,128)} %param.12) | copy-start | bytes 3076
  70.5 46.7 %copy-start.6 = (f32[1,4,64]{2,1,0:T(4,128)S(1)}, f32[1,4,64]{2,1,0:T(4,128)}, u32[]{:S(2)}) copy-start(f32[1,4,64]{2,1,0:T(4,128)} %param.13) | copy-start | bytes 3076
  70.5 51.7 %copy-start.1 = (bf16[1,4,64,1024]{3,2,1,0:T(8,128)(2,1)S(1)}, bf16[1,4,64,1024]{3,2,1,0:T(8,128)(2,1)}, u32[]{:S(2)}) copy-start(bf16[1,4,64,1024]{3,2,1,0:T(8,128)(2,1)} %param.10) | copy-start | bytes 1572868
  72.5 6.3 %collective-permute-start.3 = (bf16[64,1024]{1,0:T(8,128)(2,1)S(1)}, bf16[64,1024]{1,0:T(8,128)(2,1)S(1)}, u32[]{:S(2)}, u32[]{:S(2)}) collective-permute-start(bf16[64,1024]{1,0:T(8,128)(2,1)S(1)} %get-tuple-element.39), channel_id=1, source_target_pairs={{0,8},{8,0},{16,24},{24,16},{1,9},{9,1},{17,25},{25,17},{2,10},{10... | collective-permute-start | bytes 393224 | tf_op jit(solution)/shard_map/ppermute | solution.py:238
  73.0 6.4 %collective-permute-start.10 = (bf16[64,1024]{1,0:T(8,128)(2,1)S(1)}, bf16[64,1024]{1,0:T(8,128)(2,1)S(1)}, u32[]{:S(2)}, u32[]{:S(2)}) collective-permute-start(bf16[64,1024]{1,0:T(8,128)(2,1)S(1)} %get-tuple-element.38.refs_0_), channel_id=1, source_target_pairs={{0,4},{2,6},{4,0},{6,2},{1,5},{3,7},{5,1},{7,3},{8,12},{10,14},{12... | collective-permute-start | bytes 393224 | tf_op jit(solution)/shard_map/ppermute | solution.py:238
  73.6 5.8 %collective-permute-start.6 = (bf16[64,1024]{1,0:T(8,128)(2,1)S(1)}, bf16[64,1024]{1,0:T(8,128)(2,1)S(1)}, u32[]{:S(2)}, u32[]{:S(2)}) collective-permute-start(bf16[64,1024]{1,0:T(8,128)(2,1)S(1)} %get-tuple-element.38.refs_0_), channel_id=1, source_target_pairs={{0,2},{2,0},{4,6},{6,4},{1,3},{3,1},{5,7},{7,5},{8,10},{10,8},{12,... | collective-permute-start | bytes 393224 | tf_op jit(solution)/shard_map/ppermute | solution.py:238
  74.2 12.0 %collective-permute-start.4 = (bf16[64,1024]{1,0:T(8,128)(2,1)S(1)}, bf16[64,1024]{1,0:T(8,128)(2,1)S(1)}, u32[]{:S(2)}, u32[]{:S(2)}) collective-permute-start(bf16[64,1024]{1,0:T(8,128)(2,1)S(1)} %get-tuple-element.40), channel_id=1, source_target_pairs={{0,16},{8,24},{16,0},{24,8},{1,17},{9,25},{17,1},{25,9},{2,18},{10... | collective-permute-start | bytes 393224 | tf_op jit(solution)/shard_map/ppermute | solution.py:238
  78.8 7.4 %collective-permute-start.7 = (bf16[64,1024]{1,0:T(8,128)(2,1)S(1)}, bf16[64,1024]{1,0:T(8,128)(2,1)S(1)}, u32[]{:S(2)}, u32[]{:S(2)}) collective-permute-start(bf16[64,1024]{1,0:T(8,128)(2,1)S(1)} %collective-permute-done.3.refs_1_), channel_id=1, source_target_pairs={{0,2},{2,0},{4,6},{6,4},{1,3},{3,1},{5,7},{7,5},{8,10},{10,8},{12,... | collective-permute-start | bytes 393224 | tf_op jit(solution)/shard_map/ppermute | solution.py:238
  79.3 10.4 %collective-permute-start.5 = (bf16[64,1024]{1,0:T(8,128)(2,1)S(1)}, bf16[64,1024]{1,0:T(8,128)(2,1)S(1)}, u32[]{:S(2)}, u32[]{:S(2)}) collective-permute-start(bf16[64,1024]{1,0:T(8,128)(2,1)S(1)} %get-tuple-element.41), channel_id=1, source_target_pairs={{0,24},{8,16},{16,8},{24,0},{1,25},{9,17},{17,9},{25,1},{2,26},{10... | collective-permute-start | bytes 393224 | tf_op jit(solution)/shard_map/ppermute | solution.py:238
  79.4 8.2 %collective-permute-start.8 = (bf16[64,1024]{1,0:T(8,128)(2,1)S(1)}, bf16[64,1024]{1,0:T(8,128)(2,1)S(1)}, u32[]{:S(2)}, u32[]{:S(2)}) collective-permute-start(bf16[64,1024]{1,0:T(8,128)(2,1)S(1)} %collective-permute-done.6.refs_4_), channel_id=1, source_target_pairs={{0,4},{2,6},{4,0},{6,2},{1,5},{3,7},{5,1},{7,3},{8,12},{10,14},{12... | collective-permute-start | bytes 393224 | tf_op jit(solution)/shard_map/ppermute | solution.py:238
  80.9 6.7 %collective-permute-start.11 = (bf16[64,1024]{1,0:T(8,128)(2,1)S(1)}, bf16[64,1024]{1,0:T(8,128)(2,1)S(1)}, u32[]{:S(2)}, u32[]{:S(2)}) collective-permute-start(bf16[64,1024]{1,0:T(8,128)(2,1)S(1)} %collective-permute-done.3.refs_1_), channel_id=1, source_target_pairs={{0,4},{2,6},{4,0},{6,2},{1,5},{3,7},{5,1},{7,3},{8,12},{10,14},{12... | collective-permute-start | bytes 393224 | tf_op jit(solution)/shard_map/ppermute | solution.py:238
  86.2 6.4 %collective-permute-start.14 = (bf16[64,1024]{1,0:T(8,128)(2,1)S(1)}, bf16[64,1024]{1,0:T(8,128)(2,1)S(1)}, u32[]{:S(2)}, u32[]{:S(2)}) collective-permute-start(bf16[64,1024]{1,0:T(8,128)(2,1)S(1)} %collective-permute-done.4.refs_2_), channel_id=1, source_target_pairs={{0,4},{2,6},{4,0},{6,2},{1,5},{3,7},{5,1},{7,3},{8,12},{10,14},{12... | collective-permute-start | bytes 393224 | tf_op jit(solution)/shard_map/ppermute | solution.py:238
  87.6 6.4 %collective-permute-start.12 = (bf16[64,1024]{1,0:T(8,128)(2,1)S(1)}, bf16[64,1024]{1,0:T(8,128)(2,1)S(1)}, u32[]{:S(2)}, u32[]{:S(2)}) collective-permute-start(bf16[64,1024]{1,0:T(8,128)(2,1)S(1)} %collective-permute-done.11.refs_9_), channel_id=1, source_target_pairs={{0,2},{2,0},{4,6},{6,4},{1,3},{3,1},{5,7},{7,5},{8,10},{10,8},{12,... | collective-permute-start | bytes 393224 | tf_op jit(solution)/shard_map/ppermute | solution.py:238
  89.1 6.3 %collective-permute-start.9 = (bf16[64,1024]{1,0:T(8,128)(2,1)S(1)}, bf16[64,1024]{1,0:T(8,128)(2,1)S(1)}, u32[]{:S(2)}, u32[]{:S(2)}) collective-permute-start(bf16[64,1024]{1,0:T(8,128)(2,1)S(1)} %collective-permute-done.4.refs_2_), channel_id=1, source_target_pairs={{0,2},{2,0},{4,6},{6,4},{1,3},{3,1},{5,7},{7,5},{8,10},{10,8},{12,... | collective-permute-start | bytes 393224 | tf_op jit(solution)/shard_map/ppermute | solution.py:238
  92.6 5.0 %collective-permute-start.15 = (bf16[64,1024]{1,0:T(8,128)(2,1)S(1)}, bf16[64,1024]{1,0:T(8,128)(2,1)S(1)}, u32[]{:S(2)}, u32[]{:S(2)}) collective-permute-start(bf16[64,1024]{1,0:T(8,128)(2,1)S(1)} %collective-permute-done.5.refs_3_), channel_id=1, source_target_pairs={{0,4},{2,6},{4,0},{6,2},{1,5},{3,7},{5,1},{7,3},{8,12},{10,14},{12... | collective-permute-start | bytes 393224 | tf_op jit(solution)/shard_map/ppermute | solution.py:238
  94.0 5.0 %collective-permute-start.13 = (bf16[64,1024]{1,0:T(8,128)(2,1)S(1)}, bf16[64,1024]{1,0:T(8,128)(2,1)S(1)}, u32[]{:S(2)}, u32[]{:S(2)}) collective-permute-start(bf16[64,1024]{1,0:T(8,128)(2,1)S(1)} %collective-permute-done.5.refs_3_), channel_id=1, source_target_pairs={{0,2},{2,0},{4,6},{6,4},{1,3},{3,1},{5,7},{7,5},{8,10},{10,8},{12,... | collective-permute-start | bytes 393224 | tf_op jit(solution)/shard_map/ppermute | solution.py:238
  95.4 5.0 %collective-permute-start.16 = (bf16[64,1024]{1,0:T(8,128)(2,1)S(1)}, bf16[64,1024]{1,0:T(8,128)(2,1)S(1)}, u32[]{:S(2)}, u32[]{:S(2)}) collective-permute-start(bf16[64,1024]{1,0:T(8,128)(2,1)S(1)} %collective-permute-done.9.refs_6_), channel_id=1, source_target_pairs={{0,4},{2,6},{4,0},{6,2},{1,5},{3,7},{5,1},{7,3},{8,12},{10,14},{12... | collective-permute-start | bytes 393224 | tf_op jit(solution)/shard_map/ppermute | solution.py:238
  97.5 5.0 %collective-permute-start.17 = (bf16[64,1024]{1,0:T(8,128)(2,1)S(1)}, bf16[64,1024]{1,0:T(8,128)(2,1)S(1)}, u32[]{:S(2)}, u32[]{:S(2)}) collective-permute-start(bf16[64,1024]{1,0:T(8,128)(2,1)S(1)} %collective-permute-done.15.refs_11_), channel_id=1, source_target_pairs={{0,2},{2,0},{4,6},{6,4},{1,3},{3,1},{5,7},{7,5},{8,10},{10,8},{12,... | collective-permute-start | bytes 393224 | tf_op jit(solution)/shard_map/ppermute | solution.py:238
  112.7 6.4 %collective-permute-start.18 = (bf16[64,1024]{1,0:T(8,128)(2,1)S(1)}, bf16[64,1024]{1,0:T(8,128)(2,1)S(1)}, u32[]{:S(2)}, u32[]{:S(2)}) collective-permute-start(bf16[64,1024]{1,0:T(8,128)(2,1)S(1)} %get-tuple-element.48), channel_id=1, source_target_pairs={{0,8},{8,0},{16,24},{24,16},{1,9},{9,1},{17,25},{25,17},{2,10},{10... | collective-permute-start | bytes 393224 | tf_op jit(solution)/shard_map/ppermute | solution.py:238
  112.8 6.4 %collective-permute-start.19 = (bf16[64,1024]{1,0:T(8,128)(2,1)S(1)}, bf16[64,1024]{1,0:T(8,128)(2,1)S(1)}, u32[]{:S(2)}, u32[]{:S(2)}) collective-permute-start(bf16[64,1024]{1,0:T(8,128)(2,1)S(1)} %get-tuple-element.49), channel_id=1, source_target_pairs={{0,16},{8,24},{16,0},{24,8},{1,17},{9,25},{17,1},{25,9},{2,18},{10... | collective-permute-start | bytes 393224 | tf_op jit(solution)/shard_map/ppermute | solution.py:238
  115.3 6.9 %collective-permute-start.20 = (bf16[64,1024]{1,0:T(8,128)(2,1)S(1)}, bf16[64,1024]{1,0:T(8,128)(2,1)S(1)}, u32[]{:S(2)}, u32[]{:S(2)}) collective-permute-start(bf16[64,1024]{1,0:T(8,128)(2,1)S(1)} %get-tuple-element.50), channel_id=1, source_target_pairs={{0,24},{8,16},{16,8},{24,0},{1,25},{9,17},{17,9},{25,1},{2,26},{10... | collective-permute-start | bytes 393224 | tf_op jit(solution)/shard_map/ppermute | solution.py:238
